TPU v7x, 32 devices: a whole 2x2x4 slice. The times are simulated.
32 devices in a mesh: role: 2 (over core), dp: 4 (over z), mp: 4 (over y, x).
Axes of the slice: x: 2, y: 2, z: 4, core: 2. Of those that a mesh axis runs over, the one named last changes fastest.
Arguments:
- pixels: bfloat16 [32, 196, 768], P('dp', None, 'mp'), may hold values from -6 to 6
- context_slots: int32 [32, 160], P('dp'), may hold values from 0 to 195, as said below
- context_count: int32 [32], P('dp'), may hold values from 40 to 160
- target_slots: int32 [32, 4, 64], P('dp'), may hold values from 0 to 195, as said below
- target_count: int32 [32, 4], P('dp'), may hold values from 16 to 64
- encoder_in: float32 [768, 5376], P(('role', 'dp'), 'mp'), may hold values from -0.21875 to 0.21875
- encoder_out: float32 [4608, 768], P('mp', ('role', 'dp')), may hold values from -0.21875 to 0.21875
- predictor_in: float32 [384, 3456], P(('role', 'dp'), 'mp'), may hold values from -0.3125 to 0.3125
- predictor_out: float32 [2688, 384], P('mp', ('role', 'dp')), may hold values from -0.3125 to 0.3125
- vectors: float32 [3072], P(('role', 'dp', 'mp')), may hold values from 0.5 to 1.5
- first_encoder_in: float32 [768, 5376], P(('role', 'dp'), 'mp'), may hold values from -1.9073486e-05 to 1.9073486e-05
- first_encoder_out: float32 [4608, 768], P('mp', ('role', 'dp')), may hold values from -1.9073486e-05 to 1.9073486e-05
- first_predictor_in: float32 [384, 3456], P(('role', 'dp'), 'mp'), may hold values from -1.9073486e-05 to 1.9073486e-05
- first_predictor_out: float32 [2688, 384], P('mp', ('role', 'dp')), may hold values from -1.9073486e-05 to 1.9073486e-05
- first_vectors: float32 [3072], P(('role', 'dp', 'mp')), may hold values from -6.1035156e-05 to 6.1035156e-05
- second_encoder_in: float32 [768, 5376], P(('role', 'dp'), 'mp'), may hold values from 9.97001e-13 to 3.988004e-12
- second_encoder_out: float32 [4608, 768], P('mp', ('role', 'dp')), may hold values from 9.97001e-13 to 3.988004e-12
- second_predictor_in: float32 [384, 3456], P(('role', 'dp'), 'mp'), may hold values from 9.97001e-13 to 3.988004e-12
- second_predictor_out: float32 [2688, 384], P('mp', ('role', 'dp')), may hold values from 9.97001e-13 to 3.988004e-12
- second_vectors: float32 [3072], P(('role', 'dp', 'mp')), may hold values from 8.973009e-12 to 3.5892036e-11
- target_encoder_in: float32 [768, 5376], P(('role', 'dp'), 'mp'), may hold values from -0.21875 to 0.21875
- target_encoder_out: float32 [4608, 768], P('mp', ('role', 'dp')), may hold values from -0.21875 to 0.21875
- target_vectors: float32 [3072], P(('role', 'dp', 'mp')), may hold values from 0.5 to 1.5
Outputs:
- new_encoder_in: float32 [768, 5376], P(('role', 'dp'), 'mp')
- new_encoder_out: float32 [4608, 768], P('mp', ('role', 'dp'))
- new_predictor_in: float32 [384, 3456], P(('role', 'dp'), 'mp')
- new_predictor_out: float32 [2688, 384], P('mp', ('role', 'dp'))
- new_vectors: float32 [3072], P(('role', 'dp', 'mp'))
- new_first_encoder_in: float32 [768, 5376], P(('role', 'dp'), 'mp')
- new_first_encoder_out: float32 [4608, 768], P('mp', ('role', 'dp'))
- new_first_predictor_in: float32 [384, 3456], P(('role', 'dp'), 'mp')
- new_first_predictor_out: float32 [2688, 384], P('mp', ('role', 'dp'))
- new_first_vectors: float32 [3072], P(('role', 'dp', 'mp'))
- new_second_encoder_in: float32 [768, 5376], P(('role', 'dp'), 'mp')
- new_second_encoder_out: float32 [4608, 768], P('mp', ('role', 'dp'))
- new_second_predictor_in: float32 [384, 3456], P(('role', 'dp'), 'mp')
- new_second_predictor_out: float32 [2688, 384], P('mp', ('role', 'dp'))
- new_second_vectors: float32 [3072], P(('role', 'dp', 'mp'))
- new_target_encoder_in: float32 [768, 5376], P(('role', 'dp'), 'mp')
- new_target_encoder_out: float32 [4608, 768], P('mp', ('role', 'dp'))
- new_target_vectors: float32 [3072], P(('role', 'dp', 'mp'))
- loss_total: float32 [], replicated
- target_total: float32 [], replicated
- grad_norm: float32 [], replicated
Inputs may be any that keep to these rules, and one draw needn't show every extreme that they name: `context_slots`: each row holds distinct patch numbers; an image's context is its first context_count entries. `target_slots`: each block's row holds distinct patch numbers; a block is its first target_count entries.
All inputs are finite; a program needn't handle non-finite values.
Results may differ from a plain program's by a relative error of at most 0.0024.
The roundings to bfloat16 on the way count: a program that leaves them out, or rounds other values in their place, can miss the bound.
Values may be sent and summed in bfloat16 or wider, within the bound.
A program may use at most 320 MiB of HBM per device.

v0:
```python
import jax
import jax.numpy as jnp
from jax import lax
from jax.sharding import PartitionSpec as P

HEADS = 12
GRID = 14
STEP = 10


BETA_ONE = 0.9
BETA_TWO = 0.999
ADAM_EPS = 1e-08
RATE_MATRIX = 0.03
RATE_VECTOR = 0.3
DECAY = 0.05
MOMENTUM_EMA = 0.9
CLIP = 0.1
ROOT_HALF = 0.7071067811865476
INVERSE_ROOT = 0.3989422804014327


def from_behind(value, axis, by):
    size = lax.axis_size(axis)
    pairs = [(i, i + by) for i in range(size) if 0 <= i + by < size]
    return lax.ppermute(value, axis, pairs)


def product(left, right):
    return jnp.dot(left, right, preferred_element_type=jnp.float32)


def left_product(left, right):
    return lax.dot_general(
        left, right, (((0,), (0,)), ((), ())), preferred_element_type=jnp.float32
    )


def right_product(left, right):
    return lax.dot_general(
        left, right, (((1,), (1,)), ((), ())), preferred_element_type=jnp.float32
    )


def widen(rows):
    return lax.all_gather(rows, "mp", axis=0, tiled=True)


def narrow(terms):
    return lax.psum_scatter(terms, "mp", scatter_dimension=0, tiled=True)


def context_total(terms):
    return lax.psum(terms, "mp")


def sincos(width):
    quarter = width // 4
    omega = 1.0 / 10000.0 ** (jnp.arange(quarter).astype(jnp.float32) / quarter)
    place = jnp.arange(GRID * GRID)
    rows = (place // GRID).astype(jnp.float32)[:, None] * omega[None, :]
    cols = (place % GRID).astype(jnp.float32)[:, None] * omega[None, :]
    return jnp.concatenate([jnp.sin(rows), jnp.cos(rows), jnp.sin(cols), jnp.cos(cols)], -1)


def layer_stats(stream):
    mean = jnp.mean(stream, -1, keepdims=True)
    cent = stream - mean
    scale = lax.rsqrt(jnp.mean(cent * cent, -1, keepdims=True) + 1e-06)
    return (cent * scale, scale)


def norm_back(normed, scale, gain, grad):
    gain_grad = jnp.sum(grad * normed, 0)
    scaled = grad * gain
    inner = (
        scaled
        - jnp.mean(scaled, -1, keepdims=True)
        - normed * jnp.mean(scaled * normed, -1, keepdims=True)
    )
    return (scale * inner, gain_grad)


def gelu_slope(hidden):
    return (
        0.5 * (1.0 + lax.erf(hidden * ROOT_HALF))
        + hidden * jnp.exp(-0.5 * hidden * hidden) * INVERSE_ROOT
    )


def scores(queries, keyset, keep, size):
    raw = jnp.einsum("blhd,bmhd->bhlm", queries, keyset, preferred_element_type=jnp.float32)
    return raw * size ** (-0.5) + (keep[:, None, None, :] - 1.0) * 1000000000.0


def block_forward(stream, keep, weights, gains, length):
    w_qkv, w_up, w_out, w_down = weights
    first, second = gains
    local = w_out.shape[0]
    heads = HEADS // lax.axis_size("mp")
    size = local // heads
    first_norm, first_scale = layer_stats(stream)
    mixer_in = widen((first_norm * first).astype(jnp.bfloat16))
    rows = mixer_in.shape[0]
    seqs = rows // length
    triple = product(mixer_in, w_qkv).astype(jnp.bfloat16).reshape(seqs, length, 3, heads, size)
    queries, keyset, values = (triple[:, :, 0], triple[:, :, 1], triple[:, :, 2])
    score = scores(queries, keyset, keep, size)
    logsum = jax.nn.logsumexp(score, -1)
    probs = jnp.exp(score - logsum[..., None]).astype(jnp.bfloat16)
    mixed = jnp.einsum("bhlm,bmhd->blhd", probs, values, preferred_element_type=jnp.float32)
    mixed = mixed.astype(jnp.bfloat16).reshape(rows, local)
    middle = stream + narrow(product(mixed, w_out))
    second_norm, second_scale = layer_stats(middle)
    dense_in = widen((second_norm * second).astype(jnp.bfloat16))
    hidden = product(dense_in, w_up)
    active = jax.nn.gelu(hidden, approximate=False).astype(jnp.bfloat16)
    result = middle + narrow(product(active, w_down))
    saved = (
        first_norm,
        first_scale,
        mixer_in,
        queries,
        keyset,
        values,
        logsum,
        mixed,
        second_norm,
        second_scale,
        dense_in,
        hidden,
        active,
    )
    return (result, saved)


def block_backward(grad_out, saved, keep, weights, gains, length):
    (
        first_norm,
        first_scale,
        mixer_in,
        queries,
        keyset,
        values,
        logsum,
        mixed,
        second_norm,
        second_scale,
        dense_in,
        hidden,
        active,
    ) = saved
    w_qkv, w_up, w_out, w_down = weights
    first, second = gains
    seqs, _, heads, size = queries.shape
    rows = mixer_in.shape[0]
    grad_branch = widen(grad_out.astype(jnp.bfloat16))
    g_down = left_product(active, grad_branch)
    grad_active = right_product(grad_branch, w_down)
    grad_hidden = (grad_active * gelu_slope(hidden)).astype(jnp.bfloat16)
    g_up = left_product(dense_in, grad_hidden)
    grad_mid_norm, g_second = norm_back(
        second_norm, second_scale, second, narrow(right_product(grad_hidden, w_up))
    )
    grad_mid = grad_out + grad_mid_norm
    grad_mixer = widen(grad_mid.astype(jnp.bfloat16))
    g_out = left_product(mixed, grad_mixer)
    grad_mixed = (
        right_product(grad_mixer, w_out).astype(jnp.bfloat16).reshape(seqs, length, heads, size)
    )
    probs = jnp.exp(scores(queries, keyset, keep, size) - logsum[..., None])
    grad_probs = jnp.einsum(
        "blhd,bmhd->bhlm", grad_mixed, values, preferred_element_type=jnp.float32
    )
    grad_values = jnp.einsum(
        "bhlm,blhd->bmhd",
        probs.astype(jnp.bfloat16),
        grad_mixed,
        preferred_element_type=jnp.float32,
    ).astype(jnp.bfloat16)
    grad_scores = (probs * (grad_probs - jnp.sum(grad_probs * probs, -1, keepdims=True))).astype(
        jnp.bfloat16
    )
    grad_queries = (
        jnp.einsum("bhlm,bmhd->blhd", grad_scores, keyset, preferred_element_type=jnp.float32)
        * size ** (-0.5)
    ).astype(jnp.bfloat16)
    grad_keys = (
        jnp.einsum("bhlm,blhd->bmhd", grad_scores, queries, preferred_element_type=jnp.float32)
        * size ** (-0.5)
    ).astype(jnp.bfloat16)
    grad_triple = jnp.stack([grad_queries, grad_keys, grad_values], 2).reshape(
        rows, 3 * heads * size
    )
    g_qkv = left_product(mixer_in, grad_triple)
    grad_in_norm, g_first = norm_back(
        first_norm, first_scale, first, narrow(right_product(grad_triple, w_qkv))
    )
    return (grad_mid + grad_in_norm, (g_qkv, g_up, g_out, g_down), (g_first, g_second))


def adamw(weight, grad, first, second, scale, rate, decay):
    grad = grad * scale
    first = BETA_ONE * first + (1.0 - BETA_ONE) * grad
    second = BETA_TWO * second + (1.0 - BETA_TWO) * grad * grad
    mean_hat = first / (1.0 - BETA_ONE**STEP)
    square_hat = second / (1.0 - BETA_TWO**STEP)
    return (
        weight - rate * (mean_hat / (jnp.sqrt(square_hat) + ADAM_EPS) + decay * weight),
        first,
        second,
    )


def per_device(
    pixels,
    context_slots,
    context_count,
    target_slots,
    target_count,
    encoder_in,
    encoder_out,
    predictor_in,
    predictor_out,
    vectors,
    first_encoder_in,
    first_encoder_out,
    first_predictor_in,
    first_predictor_out,
    first_vectors,
    second_encoder_in,
    second_encoder_out,
    second_predictor_in,
    second_predictor_out,
    second_vectors,
    target_encoder_in,
    target_encoder_out,
    target_vectors,
):
    parts = lax.axis_size("mp")
    here = lax.axis_index("mp")
    student = (lax.axis_index("role") == 1).astype(jnp.float32)
    bf = jnp.bfloat16
    s_in, s_out, s_pin, s_pout, e_in, e_out = (
        lax.all_gather(encoder_in.astype(bf), ("role", "dp"), axis=0, tiled=True),
        lax.all_gather(encoder_out.astype(bf), ("role", "dp"), axis=1, tiled=True),
        lax.all_gather(predictor_in.astype(bf), ("role", "dp"), axis=0, tiled=True),
        lax.all_gather(predictor_out.astype(bf), ("role", "dp"), axis=1, tiled=True),
        lax.all_gather(target_encoder_in.astype(bf), ("role", "dp"), axis=0, tiled=True),
        lax.all_gather(target_encoder_out.astype(bf), ("role", "dp"), axis=1, tiled=True),
    )
    w_in = jnp.where(student > 0, s_in, e_in)
    w_out = jnp.where(student > 0, s_out, e_out)
    s_vec, e_vec = (
        lax.all_gather(vectors.astype(bf), ("role", "dp", "mp"), axis=0, tiled=True),
        lax.all_gather(target_vectors.astype(bf), ("role", "dp", "mp"), axis=0, tiled=True),
    )
    width = w_out.shape[1]
    pwidth = s_pin.shape[0]
    local = width // parts
    plocal = pwidth // parts
    pixel = pixels.shape[2]
    phidden = s_pin.shape[1] - 3 * plocal - local
    enc_gains = jnp.where(student > 0, s_vec[: 2 * width], e_vec[: 2 * width]).astype(jnp.float32)
    pred_gains = s_vec[2 * width :].astype(jnp.float32)
    enc_weights = (
        w_in[:, : 3 * local],
        w_in[:, 3 * local :],
        w_out[pixel : pixel + local],
        w_out[pixel + local :],
    )
    embed = w_out[:pixel]
    pred_weights = (
        s_pin[:, : 3 * plocal],
        s_pin[:, 3 * plocal : 3 * plocal + phidden],
        s_pout[local : local + plocal],
        s_pout[local + plocal :],
    )
    head = s_pin[:, 3 * plocal + phidden :]
    proj_in = s_pout[:local]
    enc_pair = (enc_gains[:width], enc_gains[width:])
    pred_pair = (pred_gains[:pwidth], pred_gains[pwidth : 2 * pwidth])
    final_gain = pred_gains[2 * pwidth : 3 * pwidth]
    mask_token = pred_gains[3 * pwidth :]
    images, patches = (pixels.shape[0], pixels.shape[1])
    slots, blocks, tslots = (context_slots.shape[1], target_slots.shape[1], target_slots.shape[2])
    length = slots + tslots
    rows = images * patches
    local_rows = rows // parts
    image_ids = jnp.arange(images)
    pix_flat = pixels.reshape(rows, pixel)
    pos_rows = lax.dynamic_slice_in_dim(
        jnp.tile(sincos(width), (images, 1)), here * local_rows, local_rows, 0
    )
    context_keep = (jnp.arange(slots)[None, :] < context_count[:, None]).astype(jnp.float32)
    hits = (context_slots[:, :, None] == jnp.arange(patches)[None, None, :]).astype(jnp.float32)
    context_mask = jnp.sum(hits * context_keep[:, :, None], 1)
    enc_keep = jnp.where(student > 0, context_mask, jnp.ones_like(context_mask))
    start = narrow(product(pix_flat, embed)) + pos_rows
    latent, enc_saved = block_forward(start, enc_keep, enc_weights, enc_pair, patches)
    normed, _ = layer_stats(latent)
    sent = jnp.where(student > 0, latent, normed).astype(bf)
    full = widen(sent).reshape(images, patches, width)
    context = lax.dynamic_slice_in_dim(
        full[image_ids[:, None], context_slots], here * local, local, 2
    )
    chosen = lax.dynamic_slice_in_dim(
        full[image_ids[:, None, None], target_slots], here * local, local, 3
    )
    chosen = jnp.transpose(chosen, (1, 0, 2, 3))
    pred_targets = from_behind(chosen, "role", 1)
    pred_keep = (jnp.arange(slots)[None, :] < context_count[:, None]).astype(jnp.float32)
    table = sincos(pwidth)
    context_flat = context.reshape(images * slots, local)
    entry = (
        context_total(product(context_flat, proj_in)).reshape(images, slots, pwidth)
        + table[context_slots]
    )
    mine = blocks // parts
    my_slots = jnp.transpose(
        lax.dynamic_slice_in_dim(target_slots, here * mine, mine, 1), (1, 0, 2)
    )
    tgt_in = mask_token + table[my_slots]
    seq = jnp.concatenate([entry[None], tgt_in], 2).reshape(-1, pwidth)
    tkeep = jnp.transpose(
        (jnp.arange(tslots)[None, None, :] < target_count[:, :, None]).astype(jnp.float32),
        (1, 0, 2),
    )
    keys_full = jnp.concatenate(
        [jnp.broadcast_to(pred_keep[None], (blocks, images, slots)), tkeep], 2
    )
    keys_full = keys_full.reshape(blocks * images, length)
    out, pred_saved = block_forward(seq, keys_full, pred_weights, pred_pair, length)
    target_rows = out.reshape(mine, images, length, pwidth)[:, :, slots:].reshape(-1, pwidth)
    final_norm, final_scale = layer_stats(target_rows)
    head_in = widen((final_norm * final_gain).astype(bf))
    pred = product(head_in, head)
    weight = tkeep.reshape(-1)[:, None] * student
    diff = pred - pred_targets.reshape(-1, local).astype(jnp.float32)
    loss_part = jnp.sum(weight * diff * diff)
    count_part = student * jnp.sum(target_count).astype(jnp.float32) / parts
    loss_total, target_total = lax.psum((loss_part, count_part), ("role", "dp", "mp"))
    grad_pred = (2.0 * weight * diff / target_total).astype(bf)
    g_head = left_product(head_in, grad_pred)
    grad_final = narrow(right_product(grad_pred, head))
    grad_rows, g_final = norm_back(final_norm, final_scale, final_gain, grad_final)
    grad_seq = jnp.concatenate(
        [
            jnp.zeros((mine, images, slots, pwidth), jnp.float32),
            grad_rows.reshape(mine, images, tslots, pwidth),
        ],
        2,
    ).reshape(-1, pwidth)
    grad_in, pred_grads, pred_gain_grads = block_backward(
        grad_seq, pred_saved, keys_full, pred_weights, pred_pair, length
    )
    grad_in = grad_in.reshape(mine, images, length, pwidth)
    g_mask = jnp.sum(grad_in[:, :, slots:], (0, 1, 2))
    grad_entry = context_total(jnp.sum(grad_in[:, :, :slots], 0).reshape(-1, pwidth)).astype(bf)
    g_proj_in = left_product(context_flat, grad_entry)
    grad_context = product(grad_entry, proj_in.T).reshape(images, slots, local)
    grad_full = (
        jnp.zeros((images, patches, local), jnp.float32)
        .at[image_ids[:, None], context_slots]
        .add(grad_context)
    )
    select = (jnp.arange(parts) == here).astype(jnp.float32)
    grad_latent = narrow(
        (grad_full[:, :, None, :] * select[None, None, :, None]).reshape(rows, parts * local)
    )
    grad_start, enc_grads, enc_gain_grads = block_backward(
        grad_latent, enc_saved, enc_keep, enc_weights, enc_pair, patches
    )
    g_embed = left_product(pix_flat, widen(grad_start.astype(bf)))
    g_in = jnp.concatenate([enc_grads[0], enc_grads[1]], 1)
    g_out = jnp.concatenate([g_embed, enc_grads[2], enc_grads[3]], 0)
    g_pin = jnp.concatenate([pred_grads[0], pred_grads[1], g_head], 1)
    g_pout = jnp.concatenate([g_proj_in, pred_grads[2], pred_grads[3]], 0)
    g_vec = jnp.concatenate(
        [
            enc_gain_grads[0],
            enc_gain_grads[1],
            pred_gain_grads[0],
            pred_gain_grads[1],
            g_final,
            g_mask,
        ]
    )
    r_in, r_out, r_pin, r_pout = (
        lax.psum_scatter(g_in, ("role", "dp"), scatter_dimension=0, tiled=True),
        lax.psum_scatter(g_out, ("role", "dp"), scatter_dimension=1, tiled=True),
        lax.psum_scatter(g_pin, ("role", "dp"), scatter_dimension=0, tiled=True),
        lax.psum_scatter(g_pout, ("role", "dp"), scatter_dimension=1, tiled=True),
    )
    r_vec = lax.psum_scatter(g_vec, ("role", "dp", "mp"), scatter_dimension=0, tiled=True)
    squares = (
        jnp.sum(r_in * r_in)
        + jnp.sum(r_out * r_out)
        + jnp.sum(r_pin * r_pin)
        + jnp.sum(r_pout * r_pout)
        + jnp.sum(r_vec * r_vec)
    )
    grad_norm = jnp.sqrt(lax.psum(squares, ("role", "dp", "mp")))
    scale = jnp.minimum(1.0, CLIP / (grad_norm + 1e-06))
    new_in, m_in, v_in = adamw(
        encoder_in, r_in, first_encoder_in, second_encoder_in, scale, RATE_MATRIX, DECAY
    )
    new_out, m_out, v_out = adamw(
        encoder_out, r_out, first_encoder_out, second_encoder_out, scale, RATE_MATRIX, DECAY
    )
    new_pin, m_pin, v_pin = adamw(
        predictor_in, r_pin, first_predictor_in, second_predictor_in, scale, RATE_MATRIX, DECAY
    )
    new_pout, m_pout, v_pout = adamw(
        predictor_out, r_pout, first_predictor_out, second_predictor_out, scale, RATE_MATRIX, DECAY
    )
    new_vec, m_vec, v_vec = adamw(
        vectors, r_vec, first_vectors, second_vectors, scale, RATE_VECTOR, 0.0
    )
    ema_in = MOMENTUM_EMA * target_encoder_in + (1.0 - MOMENTUM_EMA) * new_in
    ema_out = MOMENTUM_EMA * target_encoder_out + (1.0 - MOMENTUM_EMA) * new_out
    ema_vec = MOMENTUM_EMA * target_vectors + (1.0 - MOMENTUM_EMA) * new_vec
    return (
        new_in,
        new_out,
        new_pin,
        new_pout,
        new_vec,
        m_in,
        m_out,
        m_pin,
        m_pout,
        m_vec,
        v_in,
        v_out,
        v_pin,
        v_pout,
        v_vec,
        ema_in,
        ema_out,
        ema_vec,
        loss_total,
        target_total,
        grad_norm,
    )


def solution(mesh):
    return jax.shard_map(
        per_device,
        mesh=mesh,
        in_specs=(
            P("dp", None, "mp"),
            P("dp", None),
            P("dp"),
            P("dp", None, None),
            P("dp", None),
            P(("role", "dp"), "mp"),
            P("mp", ("role", "dp")),
            P(("role", "dp"), "mp"),
            P("mp", ("role", "dp")),
            P(("role", "dp", "mp")),
            P(("role", "dp"), "mp"),
            P("mp", ("role", "dp")),
            P(("role", "dp"), "mp"),
            P("mp", ("role", "dp")),
            P(("role", "dp", "mp")),
            P(("role", "dp"), "mp"),
            P("mp", ("role", "dp")),
            P(("role", "dp"), "mp"),
            P("mp", ("role", "dp")),
            P(("role", "dp", "mp")),
            P(("role", "dp"), "mp"),
            P("mp", ("role", "dp")),
            P(("role", "dp", "mp")),
        ),
        out_specs=(
            P(("role", "dp"), "mp"),
            P("mp", ("role", "dp")),
            P(("role", "dp"), "mp"),
            P("mp", ("role", "dp")),
            P(("role", "dp", "mp")),
            P(("role", "dp"), "mp"),
            P("mp", ("role", "dp")),
            P(("role", "dp"), "mp"),
            P("mp", ("role", "dp")),
            P(("role", "dp", "mp")),
            P(("role", "dp"), "mp"),
            P("mp", ("role", "dp")),
            P(("role", "dp"), "mp"),
            P("mp", ("role", "dp")),
            P(("role", "dp", "mp")),
            P(("role", "dp"), "mp"),
            P("mp", ("role", "dp")),
            P(("role", "dp", "mp")),
            P(),
            P(),
            P(),
        ),
        check_vma=False,
    )
```

profile of v0, /device:TPU:0, one launch (start us, length us, event | category | flops | bytes accessed | tf_op | source)
XLA Modules:
  0.0 2383.3 jit_solution(2007888954867113010)
XLA Ops:
  39.3 28.1 %all-gather.18.cloned.1.call-done = bf16[1152,768]{0,1:T(8,128)(2,1)} async-done(((bf16[1152,96]{0,1:T(8,128)(2,1)}), bf16[1152,768]{0,1:T(8,128)(2,1)}) %all-gather.18.cloned.1.call-update) | async-done | bytes 1769488 | tf_op jit(solution)/shard_map/all_gather | solution.py:250
  85.0 41.0 %all-reduce.11 = (bf16[3072]{0:T(1024)(128)(2,1)S(1)}, bf16[3072]{0:T(1024)(128)(2,1)S(1)}) all-reduce(bf16[3072]{0:T(1024)(128)(2,1)S(1)} %dynamic-update-slice.1, bf16[3072]{0:T(1024)(128)(2,1)S(1)} %dynamic-update-slice), channel_id=1, replica_groups=mesh['role'=2,'dp'=4,'mp'=4] {'role','dp','mp'}, use_global_device_ids=true, to_apply=%add.2 | all-reduce | flops 6144 | bytes 24576
  135.8 27.0 %all-gather.22.cloned.1.call-done = bf16[768,1344]{1,0:T(8,128)(2,1)} async-done(((bf16[96,1344]{1,0:T(8,128)(2,1)}), bf16[768,1344]{1,0:T(8,128)(2,1)}) %all-gather.22.cloned.1.call-update) | async-done | bytes 2064400 | tf_op jit(solution)/shard_map/all_gather | solution.py:245
  162.9 31.2 %all-gather.24.cloned.1.call-done = bf16[768,1344]{1,0:T(8,128)(2,1)} async-done(((bf16[96,1344]{1,0:T(8,128)(2,1)}), bf16[768,1344]{1,0:T(8,128)(2,1)}) %all-gather.24.cloned.1.call-update) | async-done | bytes 2064400 | tf_op jit(solution)/shard_map/all_gather | solution.py:249
  197.2 35.9 %all-gather.20.cloned.1.call-done = bf16[1568,768]{1,0:T(8,128)(2,1)} async-done(((bf16[392,768]{1,0:T(8,128)(2,1)}), bf16[1568,768]{1,0:T(8,128)(2,1)}) %all-gather.20.cloned.1.call-update) | async-done | bytes 2408464 | tf_op jit(solution)/shard_map/all_gather | solution.py:46
  258.6 58.0 %reduce-scatter.56.cloned.1.call-done = f32[392,768]{1,0:T(8,128)} async-done(((f32[1568,768]{1,0:T(8,128)}), f32[392,768]{1,0:T(8,128)}) %reduce-scatter.56.cloned.1.call-update) | async-done | bytes 1204240
  319.8 37.7 %all-gather.26.cloned.1.call-done = bf16[1568,768]{1,0:T(8,128)(2,1)} async-done(((bf16[392,768]{1,0:T(8,128)(2,1)}), bf16[1568,768]{1,0:T(8,128)(2,1)}) %all-gather.26.cloned.1.call-update) | async-done | bytes 2408464 | tf_op jit(solution)/shard_map/all_gather | solution.py:46
  379.8 58.0 %reduce-scatter.58.cloned.1.call-done = f32[392,768]{1,0:T(8,128)} async-done(((f32[1568,768]{1,0:T(8,128)}), f32[392,768]{1,0:T(8,128)}) %reduce-scatter.58.cloned.1.call-update) | async-done | bytes 1204240
  513.1 57.3 %all-reduce.15.cloned.1.call-done = f32[1280,384]{1,0:T(8,128)} async-done(((f32[1280,384]{1,0:T(8,128)}), f32[1280,384]{1,0:T(8,128)}) %all-reduce.15.cloned.1.call-update) | async-done | bytes 1966096 | tf_op jit(solution)/shard_map/psum | solution.py:54
  580.0 27.2 %all_gather.68 = bf16[384,864]{1,0:T(8,128)(2,1)S(1)} all-gather(bf16[48,864]{1,0:T(8,128)(2,1)S(1)} %convert_element_type.275), channel_id=1, replica_groups=mesh['role'=2,'dp'=4,'mp'=4] {'role','dp'}, dimensions={0}, use_global_device_ids=true | all-gather | bytes 746496 | tf_op jit(solution)/shard_map/all_gather | solution.py:247
  607.2 36.2 %all-gather.30.cloned.1.call-done = bf16[7168,384]{1,0:T(8,128)(2,1)} async-done(((bf16[1792,384]{1,0:T(8,128)(2,1)}), bf16[7168,384]{1,0:T(8,128)(2,1)}) %all-gather.30.cloned.1.call-update) | async-done | bytes 5505040 | tf_op jit(solution)/shard_map/all_gather | solution.py:46
  700.6 107.7 %reduce-scatter.36.cloned.1.call-done = f32[1792,384]{1,0:T(8,128)} async-done(((f32[7168,384]{1,0:T(8,128)}), f32[1792,384]{1,0:T(8,128)}) %reduce-scatter.36.cloned.1.call-update) | async-done | bytes 2752528 | tf_op jit(solution)/shard_map/reduce_scatter | solution.py:50
  814.0 63.7 %all-gather.32.cloned.1.call-done = bf16[7168,384]{1,0:T(8,128)(2,1)} async-done(((bf16[1792,384]{1,0:T(8,128)(2,1)}), bf16[7168,384]{1,0:T(8,128)(2,1)}) %all-gather.32.cloned.1.call-update) | async-done | bytes 5505040 | tf_op jit(solution)/shard_map/all_gather | solution.py:46
  877.7 29.3 %fusion.4 = (bf16[7168,384]{1,0:T(8,128)(2,1)S(1)}, f32[7168,384]{1,0:T(8,128)}) fusion(bf16[7168,384]{1,0:T(8,128)(2,1)} %all-gather.32.cloned.1.call-done, bf16[384,864]{1,0:T(8,128)(2,1)} %copy-done.38), kind=kOutput, calls=%fused_computation.16 | convolution fusion | flops 2292842496 | bytes 22315008 | tf_op jit(solution)/shard_map/dot_general | solution.py:30
  915.7 107.9 %reduce-scatter.38.cloned.1.call-done = f32[1792,384]{1,0:T(8,128)} async-done(((f32[7168,384]{1,0:T(8,128)}), f32[1792,384]{1,0:T(8,128)}) %reduce-scatter.38.cloned.1.call-update) | async-done | bytes 2752528 | tf_op jit(solution)/shard_map/reduce_scatter | solution.py:50
  1059.6 39.7 %psum.36 = f32[]{:T(128)} all-reduce(f32[]{:T(128)S(6)} %div.222), channel_id=1, replica_groups=mesh['role'=2,'dp'=4,'mp'=4] {'role','dp','mp'}, use_global_device_ids=true, to_apply=%region_24.25 | all-reduce | flops 1 | bytes 8 | tf_op jit(solution)/shard_map/psum | solution.py:342
  1110.1 44.9 %reduce-scatter.40.cloned.1.call-done = f32[512,384]{1,0:T(8,128)} async-done(((f32[2048,384]{1,0:T(8,128)}), f32[512,384]{1,0:T(8,128)}) %reduce-scatter.40.cloned.1.call-update) | async-done | bytes 786448 | tf_op jit(solution)/shard_map/reduce_scatter | solution.py:50
  1161.7 63.7 %all-gather.36.cloned.1.call-done = bf16[7168,384]{1,0:T(8,128)(2,1)} async-done(((bf16[1792,384]{1,0:T(8,128)(2,1)}), bf16[7168,384]{1,0:T(8,128)(2,1)}) %all-gather.36.cloned.1.call-update) | async-done | bytes 5505040 | tf_op jit(solution)/shard_map/all_gather | solution.py:46
  1244.2 107.9 %reduce-scatter.42.cloned.1.call-done = f32[1792,384]{1,0:T(8,128)} async-done(((f32[7168,384]{1,0:T(8,128)}), f32[1792,384]{1,0:T(8,128)}) %reduce-scatter.42.cloned.1.call-update) | async-done | bytes 2752528 | tf_op jit(solution)/shard_map/reduce_scatter | solution.py:50
  1359.3 63.5 %all-gather.38.cloned.1.call-done = bf16[7168,384]{1,0:T(8,128)(2,1)} async-done(((bf16[1792,384]{1,0:T(8,128)(2,1)}), bf16[7168,384]{1,0:T(8,128)(2,1)}) %all-gather.38.cloned.1.call-update) | async-done | bytes 5505040 | tf_op jit(solution)/shard_map/all_gather | solution.py:46
  1512.4 107.1 %reduce-scatter.44.cloned.1.call-done = f32[1792,384]{1,0:T(8,128)} async-done(((f32[7168,384]{1,0:T(8,128)}), f32[1792,384]{1,0:T(8,128)}) %reduce-scatter.44.cloned.1.call-update) | async-done | bytes 2752528 | tf_op jit(solution)/shard_map/reduce_scatter | solution.py:50
  1626.2 70.5 %all-reduce.16 = bf16[1280,384]{1,0:T(8,128)(2,1)S(1)} all-reduce(f32[1280,384]{1,0:T(8,128)S(1)} %bitcast.237), channel_id=1, replica_groups=mesh['role'=2,'dp'=4,'mp'=4] {'mp'}, use_global_device_ids=true, to_apply=%region_35.36 | all-reduce | flops 491520 | bytes 2949120 | tf_op jit(solution)/shard_map/psum | solution.py:54
  1734.3 58.1 %reduce-scatter.60.cloned.1.call-done = f32[392,768]{1,0:T(8,128)} async-done(((f32[1568,768]{1,0:T(8,128)}), f32[392,768]{1,0:T(8,128)}) %reduce-scatter.60.cloned.1.call-update) | async-done | bytes 1204240
  1794.6 38.0 %all-gather.40.cloned.1.call-done = bf16[1568,768]{1,0:T(8,128)(2,1)} async-done(((bf16[392,768]{1,0:T(8,128)(2,1)}), bf16[1568,768]{1,0:T(8,128)(2,1)}) %all-gather.40.cloned.1.call-update) | async-done | bytes 2408464 | tf_op jit(solution)/shard_map/all_gather | solution.py:46
  1844.4 58.0 %reduce-scatter.62.cloned.1.call-done = f32[392,768]{1,0:T(8,128)} async-done(((f32[1568,768]{1,0:T(8,128)}), f32[392,768]{1,0:T(8,128)}) %reduce-scatter.62.cloned.1.call-update) | async-done | bytes 1204240
  1906.2 38.0 %all-gather.42.cloned.1.call-done = bf16[1568,768]{1,0:T(8,128)(2,1)} async-done(((bf16[392,768]{1,0:T(8,128)(2,1)}), bf16[1568,768]{1,0:T(8,128)(2,1)}) %all-gather.42.cloned.1.call-update) | async-done | bytes 2408464 | tf_op jit(solution)/shard_map/all_gather | solution.py:46
  1970.9 58.0 %reduce-scatter.64.cloned.1.call-done = f32[392,768]{1,0:T(8,128)} async-done(((f32[1568,768]{1,0:T(8,128)}), f32[392,768]{1,0:T(8,128)}) %reduce-scatter.64.cloned.1.call-update) | async-done | bytes 1204240
  2112.9 35.3 %reduce-scatter.52.cloned.1.call-done = f32[48,672]{1,0:T(8,128)} async-done(((f32[384,672]{1,0:T(8,128)}), f32[48,672]{1,0:T(8,128)}) %reduce-scatter.52.cloned.1.call-update) | async-done | bytes 129040
  2150.1 91.4 %reduce-scatter.46.cloned.1.call-done = f32[96,1344]{1,0:T(8,128)} async-done(((f32[768,1344]{1,0:T(8,128)}), f32[96,1344]{1,0:T(8,128)}) %reduce-scatter.46.cloned.1.call-update) | async-done | bytes 516112 | tf_op jit(solution)/shard_map/reduce_scatter | solution.py:390
  2243.7 43.6 %all-reduce.9 = f32[3072]{0:T(1024)S(1)} all-reduce(f32[3072]{0:T(1024)S(1)} %constant_dynamic-update-slice_fusion), channel_id=17, replica_groups=mesh['role'=2,'dp'=4,'mp'=4] {'role','dp','mp'}, use_global_device_ids=true, to_apply=%region_59.60.clone | all-reduce | flops 3072 | bytes 24576
  2288.0 32.7 %reduce-scatter.48.cloned.1.call-done = f32[96,1152]{1,0:T(8,128)} async-done(((f32[768,1152]{1,0:T(8,128)}), f32[96,1152]{1,0:T(8,128)}) %reduce-scatter.48.cloned.1.call-update) | async-done | bytes 442384
  2326.0 40.0 %all-reduce.10 = (f32[]{:T(128)}, f32[]{:T(128)}) all-reduce(f32[]{:T(128)S(6)} %add.435, f32[]{:T(128)} %get-tuple-element.157), channel_id=1, replica_groups=mesh['role'=2,'dp'=4,'mp'=4] {'role','dp','mp'}, use_global_device_ids=true, to_apply=%region_61.62 | all-reduce | flops 2 | bytes 16 | tf_op jit(solution)/shard_map/psum | solution.py:403
  (566 shorter events, 624.0 us)
Async XLA Ops:
  7.2 32.1 %all-gather.16.cloned.1.call-start = ((), (), s32[]{:S(2)}) async-start(), calls=%async_computation.15 | async-start | bytes 1990656 | tf_op jit(solution)/shard_map/all_gather | solution.py:246
  9.0 58.5 %all-gather.18.cloned.1.call-start = ((), (), s32[]{:S(2)}) async-start(), calls=%async_computation.16 | async-start | bytes 1990656 | tf_op jit(solution)/shard_map/all_gather | solution.py:250
  10.8 120.4 %reduce-scatter.54.cloned.1.call-start = ((), (), s32[]{:S(2)}) async-start(), calls=%async_computation.40 | async-start | bytes 6021120
  72.3 90.6 %all-gather.22.cloned.1.call-start = ((), (), s32[]{:S(2)}) async-start(), calls=%async_computation.18 | async-start | bytes 2433024 | tf_op jit(solution)/shard_map/all_gather | solution.py:245
  74.0 120.0 %all-gather.24.cloned.1.call-start = ((), (), s32[]{:S(2)}) async-start(), calls=%async_computation.19 | async-start | bytes 2433024 | tf_op jit(solution)/shard_map/all_gather | solution.py:249
  74.9 158.3 %all-gather.20.cloned.1.call-start = ((), (), s32[]{:S(2)}) async-start(), calls=%async_computation.17 | async-start | bytes 3010560 | tf_op jit(solution)/shard_map/all_gather | solution.py:46
  134.5 182.2 %reduce-scatter.56.cloned.1.call-start = ((), (), s32[]{:S(2)}) async-start(), calls=%async_computation.41 | async-start | bytes 6021120
  258.6 99.0 %all-gather.26.cloned.1.call-start = ((), (), s32[]{:S(2)}) async-start(), calls=%async_computation.20 | async-start | bytes 3010560 | tf_op jit(solution)/shard_map/all_gather | solution.py:46
  319.5 118.3 %reduce-scatter.58.cloned.1.call-start = ((), (), s32[]{:S(2)}) async-start(), calls=%async_computation.42 | async-start | bytes 6021120
  379.8 99.0 %all-gather.28.cloned.1.call-start = ((), (), s32[]{:S(2)}) async-start(), calls=%async_computation.21 | async-start | bytes 3010560 | tf_op jit(solution)/shard_map/all_gather | solution.py:46
  440.7 129.7 %all-reduce.15.cloned.1.call-start = ((), (), s32[]{:S(2)}) async-start(), calls=%async_computation.22 | async-start | bytes 3932160 | tf_op jit(solution)/shard_map/psum | solution.py:54
  502.8 140.6 %all-gather.30.cloned.1.call-start = ((), (), s32[]{:S(2)}) async-start(), calls=%async_computation.23 | async-start | bytes 6881280 | tf_op jit(solution)/shard_map/all_gather | solution.py:46
  579.7 228.6 %reduce-scatter.36.cloned.1.call-start = ((), (), s32[]{:S(2)}) async-start(), calls=%async_computation.24 | async-start | bytes 13762560 | tf_op jit(solution)/shard_map/reduce_scatter | solution.py:50
  700.3 177.4 %all-gather.32.cloned.1.call-start = ((), (), s32[]{:S(2)}) async-start(), calls=%async_computation.25 | async-start | bytes 6881280 | tf_op jit(solution)/shard_map/all_gather | solution.py:46
  813.9 209.7 %reduce-scatter.38.cloned.1.call-start = ((), (), s32[]{:S(2)}) async-start(), calls=%async_computation.26 | async-start | bytes 13762560 | tf_op jit(solution)/shard_map/reduce_scatter | solution.py:50
  915.6 186.9 %all-gather.34.cloned.1.call-start = ((), (), s32[]{:S(2)}) async-start(), calls=%async_computation.27 | async-start | bytes 1966080 | tf_op jit(solution)/shard_map/all_gather | solution.py:46
  1027.3 127.7 %reduce-scatter.40.cloned.1.call-start = ((), (), s32[]{:S(2)}) async-start(), calls=%async_computation.28 | async-start | bytes 3932160 | tf_op jit(solution)/shard_map/reduce_scatter | solution.py:50
  1055.5 43.9 %collective-permute-start = (bf16[4,8,64,192]{3,2,1,0:T(8,128)(2,1)S(1)}, bf16[4,8,64,192]{3,2,1,0:T(8,128)(2,1)}, u32[]{:S(2)}, u32[]{:S(2)}) collective-permute-start(bf16[4,8,64,192]{3,2,1,0:T(8,128)(2,1)S(1)} %copy_bitcast_fusion.9), channel_id=1, source_target_pairs={{0,16},{1,17},{2,18},{3,19},{4,20},{5,21},{6,22},{7,23},{8,24},{9,... | collective-permute-start | bytes 2359304 | tf_op jit(solution)/shard_map/ppermute | solution.py:26
  1110.1 115.3 %all-gather.36.cloned.1.call-start = ((), (), s32[]{:S(2)}) async-start(), calls=%async_computation.29 | async-start | bytes 6881280 | tf_op jit(solution)/shard_map/all_gather | solution.py:46
  1161.6 190.5 %reduce-scatter.42.cloned.1.call-start = ((), (), s32[]{:S(2)}) async-start(), calls=%async_computation.30 | async-start | bytes 13762560 | tf_op jit(solution)/shard_map/reduce_scatter | solution.py:50
  1244.1 178.7 %all-gather.38.cloned.1.call-start = ((), (), s32[]{:S(2)}) async-start(), calls=%async_computation.31 | async-start | bytes 6881280 | tf_op jit(solution)/shard_map/all_gather | solution.py:46
  1359.1 260.4 %reduce-scatter.44.cloned.1.call-start = ((), (), s32[]{:S(2)}) async-start(), calls=%async_computation.32 | async-start | bytes 13762560 | tf_op jit(solution)/shard_map/reduce_scatter | solution.py:50
  1511.5 280.9 %reduce-scatter.60.cloned.1.call-start = ((), (), s32[]{:S(2)}) async-start(), calls=%async_computation.43 | async-start | bytes 6021120
  1734.3 98.3 %all-gather.40.cloned.1.call-start = ((), (), s32[]{:S(2)}) async-start(), calls=%async_computation.33 | async-start | bytes 3010560 | tf_op jit(solution)/shard_map/all_gather | solution.py:46
  1794.6 107.8 %reduce-scatter.62.cloned.1.call-start = ((), (), s32[]{:S(2)}) async-start(), calls=%async_computation.44 | async-start | bytes 6021120
  1844.3 99.9 %all-gather.42.cloned.1.call-start = ((), (), s32[]{:S(2)}) async-start(), calls=%async_computation.34 | async-start | bytes 3010560 | tf_op jit(solution)/shard_map/all_gather | solution.py:46
  1906.2 122.8 %reduce-scatter.64.cloned.1.call-start = ((), (), s32[]{:S(2)}) async-start(), calls=%async_computation.45 | async-start | bytes 6021120
  1970.9 114.2 %all-gather.44.cloned.1.call-start = ((), (), s32[]{:S(2)}) async-start(), calls=%async_computation.35 | async-start | bytes 3010560 | tf_op jit(solution)/shard_map/all_gather | solution.py:46
  2033.6 76.3 %reduce-scatter.50.cloned.1.call-start = ((), (), s32[]{:S(2)}) async-start(), calls=%async_computation.38 | async-start | bytes 1548288 | tf_op jit(solution)/shard_map/reduce_scatter | solution.py:392
  2047.8 100.5 %reduce-scatter.52.cloned.1.call-start = ((), (), s32[]{:S(2)}) async-start(), calls=%async_computation.39 | async-start | bytes 1327104
  2061.2 180.3 %reduce-scatter.46.cloned.1.call-start = ((), (), s32[]{:S(2)}) async-start(), calls=%async_computation.36 | async-start | bytes 4866048 | tf_op jit(solution)/shard_map/reduce_scatter | solution.py:390
  2076.2 244.5 %reduce-scatter.48.cloned.1.call-start = ((), (), s32[]{:S(2)}) async-start(), calls=%async_computation.37 | async-start | bytes 3981312
  (129 other events, 5775.8 us)
Sparse Core Ops, SparseCore 0:
  10.2 29.0 all-gather.15
  41.5 25.9 all-gather.17
  72.4 58.7 reduce-scatter.53
  133.2 29.6 all-gather.21
  164.9 29.1 all-gather.23
  195.8 37.3 all-gather.19
  258.7 57.8 reduce-scatter.55
  319.7 37.8 all-gather.25
  379.9 57.8 reduce-scatter.57
  440.9 37.8 all-gather.27
  502.9 67.4 all-reduce.14
  579.8 63.6 all-gather.29
  700.5 107.8 reduce-scatter.35
  814.1 63.5 all-gather.31
  915.7 107.8 reduce-scatter.37
  1027.4 30.9 all-gather.33
  1110.2 44.7 reduce-scatter.39
  1161.8 63.5 all-gather.35
  1244.2 107.8 reduce-scatter.41
  1359.2 63.5 all-gather.37
  1511.6 107.8 reduce-scatter.43
  1734.4 57.9 reduce-scatter.59
  1794.7 37.8 all-gather.39
  1844.4 57.8 reduce-scatter.61
  1906.3 37.8 all-gather.41
  1971.0 57.8 reduce-scatter.63
  2033.7 37.8 all-gather.43
  2073.9 35.9 reduce-scatter.49
  2112.2 35.9 reduce-scatter.51
  2150.5 90.9 reduce-scatter.45
  2243.9 76.7 reduce-scatter.47
where the time goes:
time: 2390 us; the launch traced here: 2380 us
  waiting for transfers between devices  1510 us (63%)
  blocking collectives  289 us (12%)
  matrix products  251 us (11%)
  local copies, waits for them, and re-layouts  180 us (8%)
  other arithmetic  129 us (5%)
    reduce_scatter x5, waiting for transfers between devices, narrow(): return lax.psum_scatter(terms, 'mp', scatter_dimension=0, tiled=True)  476 us
    all_gather x11, waiting for transfers between devices, widen(): return lax.all_gather(rows, 'mp', axis=0, tiled=True)  388 us
    unnamed x39, waiting for transfers between devices  364 us
    reduce_scatter x1, waiting for transfers between devices, per_device(): lax.psum_scatter(g_in, ('role', 'dp'), scatter_dimension=0, tiled=True)  91.4 us
    dot_general x12, matrix products, product(): return jnp.dot(left, right, preferred_element_type=jnp.float32)  87.9 us
    unnamed x2, blocking collectives  84.6 us
    psum x1, blocking collectives, context_total(): return lax.psum(terms, 'mp')  70.5 us
    psum x1, waiting for transfers between devices, context_total(): return lax.psum(terms, 'mp')  57.3 us
  transfers between devices with their start and end apart: 32, of which 29 were waited for; matrix products, arithmetic and copies ran while one was open for 5% of the time, Pallas kernels for 0%

commit v1 on v0

v1 whole, which is shorter than its diff:
```python
import jax
import jax.numpy as jnp
import numpy as np
from jax import lax
from jax.sharding import PartitionSpec as P

HEADS = 12
GRID = 14
STEP = 10

BETA_ONE = 0.9
BETA_TWO = 0.999
ADAM_EPS = 1e-08
RATE_MATRIX = 0.03
RATE_VECTOR = 0.3
DECAY = 0.05
MOMENTUM_EMA = 0.9
CLIP = 0.1
ROOT_HALF = 0.7071067811865476
INVERSE_ROOT = 0.3989422804014327

BF = jnp.bfloat16
F32 = jnp.float32
EVERY = ("mp", "role", "dp")


def dots(spec, left, right):
    return jnp.einsum(spec, left, right, preferred_element_type=F32)


def sincos(width):
    quarter = width // 4
    omega = 1.0 / 10000.0 ** (np.arange(quarter, dtype=np.float64) / quarter)
    place = np.arange(GRID * GRID)
    rows = (place // GRID)[:, None] * omega[None, :]
    cols = (place % GRID)[:, None] * omega[None, :]
    return np.concatenate([np.sin(rows), np.cos(rows), np.sin(cols), np.cos(cols)], -1).astype(
        np.float32
    )


def pick(table, places):
    hot = (places[:, None] == jnp.arange(table.shape[0])[None, :]).astype(F32)
    return jnp.dot(hot, table, precision=lax.Precision.HIGHEST, preferred_element_type=F32)


def layer_stats(stream):
    mean = jnp.mean(stream, -1, keepdims=True)
    cent = stream - mean
    scale = lax.rsqrt(jnp.mean(cent * cent, -1, keepdims=True) + 1e-06)
    return (cent * scale, scale)


def norm_back(normed, scale, gain, grad):
    gain_grad = jnp.sum(grad * normed, 0)
    scaled = grad * gain
    inner = (
        scaled
        - jnp.mean(scaled, -1, keepdims=True)
        - normed * jnp.mean(scaled * normed, -1, keepdims=True)
    )
    return (scale * inner, gain_grad)


def gelu(hidden):
    return 0.5 * hidden * (1.0 + lax.erf(hidden * ROOT_HALF))


def gelu_slope(hidden):
    return (
        0.5 * (1.0 + lax.erf(hidden * ROOT_HALF))
        + hidden * jnp.exp(-0.5 * hidden * hidden) * INVERSE_ROOT
    )


def pack_encoder(w_in, w_out, local, pixel):
    turned = w_out.T
    return jnp.concatenate(
        [
            w_in[:, : 3 * local],
            turned[:, pixel : pixel + local],
            w_in[:, 3 * local :],
            turned[:, pixel + local :],
            turned[:, :pixel],
        ],
        1,
    )


def unpack_encoder(packed, local, hidden, pixel):
    up = 4 * local
    down = up + hidden
    emb = down + hidden
    w_in = jnp.concatenate([packed[:, : 3 * local], packed[:, up:down]], 1)
    turned = jnp.concatenate(
        [packed[:, emb:], packed[:, 3 * local : up], packed[:, down:emb]], 1
    )
    return (w_in, turned.T)


def pack_predictor(p_in, p_out, local, plocal, phidden):
    turned = p_out.T
    return jnp.concatenate(
        [
            p_in[:, : 3 * plocal],
            turned[:, local : local + plocal],
            p_in[:, 3 * plocal : 3 * plocal + phidden],
            turned[:, local + plocal :],
            p_in[:, 3 * plocal + phidden :],
            turned[:, :local],
        ],
        1,
    )


def unpack_predictor(packed, local, plocal, phidden):
    up = 4 * plocal
    down = up + phidden
    head = down + phidden
    entry = head + local
    p_in = jnp.concatenate(
        [packed[:, : 3 * plocal], packed[:, up:down], packed[:, head:entry]], 1
    )
    turned = jnp.concatenate(
        [packed[:, entry:], packed[:, 3 * plocal : up], packed[:, down:head]], 1
    )
    return (p_in, turned.T)


def adamw(weight, grad, first, second, scale, rate, decay):
    grad = grad * scale
    first = BETA_ONE * first + (1.0 - BETA_ONE) * grad
    second = BETA_TWO * second + (1.0 - BETA_TWO) * grad * grad
    mean_hat = first / (1.0 - BETA_ONE**STEP)
    square_hat = second / (1.0 - BETA_TWO**STEP)
    return (
        weight - rate * (mean_hat / (jnp.sqrt(square_hat) + ADAM_EPS) + decay * weight),
        first,
        second,
    )


def split_heads(packed, heads):
    groups, rows, cols = packed.shape
    return packed.reshape(groups, rows, heads, cols // heads)


def merge_heads(split):
    groups, rows, heads, size = split.shape
    return split.reshape(groups, rows, heads * size)


def rest_forward(stream, mixed, w_o, w_up, w_down, second):
    middle = stream + dots("gnk,gdk->nd", mixed, w_o)
    norm2, scale2 = layer_stats(middle)
    dense = (norm2 * second).astype(BF)
    hidden = dots("nd,gdk->gnk", dense, w_up)
    active = gelu(hidden).astype(BF)
    out = middle + dots("gnk,gdk->nd", active, w_down)
    return (out, (norm2, scale2, dense, hidden, active))


def rest_backward(grad_out, saved, mixed, w_o, w_up, w_down, second):
    norm2, scale2, dense, hidden, active = saved
    branch = grad_out.astype(BF)
    g_down = dots("nd,gnk->gdk", branch, active)
    grad_hidden = (dots("nd,gdk->gnk", branch, w_down) * gelu_slope(hidden)).astype(BF)
    g_up = dots("nd,gnk->gdk", dense, grad_hidden)
    grad_norm, g_second = norm_back(norm2, scale2, second, dots("gnk,gdk->nd", grad_hidden, w_up))
    grad_mid = grad_out + grad_norm
    mixer = grad_mid.astype(BF)
    g_o = dots("nd,gnk->gdk", mixer, mixed)
    grad_mixed = dots("nd,gdk->gnk", mixer, w_o).astype(BF)
    return (grad_mid, grad_mixed, g_o, g_up, g_down, g_second)


def encoder_forward(pix, place, keep, bank, gains, sizes, asked):
    local, hidden, pixel = sizes
    heads = HEADS // bank.shape[0]
    size = local // heads
    up = 4 * local
    down = up + hidden
    emb = down + hidden
    start = dots("gnk,gdk->nd", pix, bank[:, :, emb:]) + place
    norm1, scale1 = layer_stats(start)
    mixer_in = (norm1 * gains[0]).astype(BF)
    triple = dots("nd,gdk->gnk", mixer_in, bank[:, :, : 3 * local]).astype(BF)
    queries = split_heads(triple[:, :asked, :local], heads)
    keyset = split_heads(triple[:, :, local : 2 * local], heads)
    values = split_heads(triple[:, :, 2 * local :], heads)
    score = dots("gnhs,gmhs->ghnm", queries, keyset) * size**-0.5 + (keep - 1.0) * 1e9
    probs32 = jax.nn.softmax(score, -1)
    probs = probs32.astype(BF)
    mixed = merge_heads(dots("ghnm,gmhs->gnhs", probs, values).astype(BF))
    out, rest = rest_forward(
        start[:asked], mixed, bank[:, :, 3 * local : up], bank[:, :, up:down],
        bank[:, :, down:emb], gains[1],
    )
    return (out, (norm1, scale1, mixer_in, queries, keyset, values, probs32, mixed, rest))


def encoder_backward(grad_out, saved, pix, bank, gains, sizes):
    norm1, scale1, mixer_in, queries, keyset, values, probs32, mixed, rest = saved
    local, hidden, pixel = sizes
    asked = queries.shape[1]
    size = queries.shape[3]
    up = 4 * local
    down = up + hidden
    emb = down + hidden
    heads = queries.shape[2]
    grad_mid, grad_mixed, g_o, g_up, g_down, g_second = rest_backward(
        grad_out, rest, mixed, bank[:, :, 3 * local : up], bank[:, :, up:down],
        bank[:, :, down:emb], gains[1],
    )
    grad_mixed = split_heads(grad_mixed, heads)
    probs = probs32.astype(BF)
    grad_probs = dots("gnhs,gmhs->ghnm", grad_mixed, values)
    grad_values = dots("ghnm,gnhs->gmhs", probs, grad_mixed).astype(BF)
    grad_scores = (
        probs32 * (grad_probs - jnp.sum(grad_probs * probs32, -1, keepdims=True))
    ).astype(BF)
    grad_queries = (dots("ghnm,gmhs->gnhs", grad_scores, keyset) * size**-0.5).astype(BF)
    grad_keys = (dots("ghnm,gnhs->gmhs", grad_scores, queries) * size**-0.5).astype(BF)
    total = mixer_in.shape[0]
    grad_queries = jnp.pad(merge_heads(grad_queries), ((0, 0), (0, total - asked), (0, 0)))
    triple = jnp.concatenate([grad_queries, merge_heads(grad_keys), merge_heads(grad_values)], 2)
    g_qkv = dots("nd,gnk->gdk", mixer_in, triple)
    grad_norm, g_first = norm_back(
        norm1, scale1, gains[0], dots("gnk,gdk->nd", triple, bank[:, :, : 3 * local])
    )
    grad_start = (jnp.pad(grad_mid, ((0, total - asked), (0, 0))) + grad_norm).astype(BF)
    g_emb = dots("nd,gnk->gdk", grad_start, pix)
    return (jnp.concatenate([g_qkv, g_o, g_up, g_down, g_emb], 2), g_first, g_second)


def predictor(context, targets, table, slots, tslots, ckeep, tkeep, total, bank, gains, sizes):
    local, plocal, phidden = sizes
    first, second, final, token = gains
    heads = HEADS // bank.shape[0]
    size = plocal // heads
    up = 4 * plocal
    down = up + phidden
    head_at = down + phidden
    entry_at = head_at + local
    w_qkv = bank[:, :, : 3 * plocal]
    w_o = bank[:, :, 3 * plocal : up]
    w_up = bank[:, :, up:down]
    w_down = bank[:, :, down:head_at]
    w_head = bank[:, :, head_at:entry_at]
    w_entry = bank[:, :, entry_at:]
    groups = bank.shape[0]
    blocks, tlen = tslots.shape
    nctx = slots.shape[0]
    asked = blocks * tlen
    spread = context.reshape(nctx, groups, local).transpose(1, 0, 2)
    entry = dots("gnk,gdk->nd", spread, w_entry) + pick(table, slots)
    tgt_in = token + pick(table, tslots.reshape(-1))
    norm1, scale1 = layer_stats(jnp.concatenate([entry, tgt_in], 0))
    mixer_in = (norm1 * first).astype(BF)
    triple = dots("nd,gdk->gnk", mixer_in, w_qkv).astype(BF)
    queries = split_heads(triple[:, nctx:, :plocal], heads)
    keyset = split_heads(triple[:, :, plocal : 2 * plocal], heads)
    values = split_heads(triple[:, :, 2 * plocal :], heads)
    shape_b = (groups, blocks, tlen, heads, size)
    q_b = queries.reshape(shape_b)
    k_c, v_c = (keyset[:, :nctx], values[:, :nctx])
    k_t, v_t = (keyset[:, nctx:].reshape(shape_b), values[:, nctx:].reshape(shape_b))
    s_c = dots("gbnhs,gmhs->ghbnm", q_b, k_c) * size**-0.5 + (ckeep - 1.0) * 1e9
    s_t = (
        dots("gbnhs,gbmhs->ghbnm", q_b, k_t) * size**-0.5 + (tkeep[:, None, :] - 1.0) * 1e9
    )
    score = jnp.concatenate([s_c, s_t], -1)
    probs32 = jax.nn.softmax(score, -1)
    probs = probs32.astype(BF)
    mixed = dots("ghbnm,gmhs->gbnhs", probs[..., :nctx], v_c) + dots(
        "ghbnm,gbmhs->gbnhs", probs[..., nctx:], v_t
    )
    mixed = mixed.astype(BF).reshape(groups, asked, plocal)
    out, rest = rest_forward(tgt_in, mixed, w_o, w_up, w_down, second)
    norm_f, scale_f = layer_stats(out)
    head_in = (norm_f * final).astype(BF)
    pred = dots("nd,gdk->gnk", head_in, w_head)
    weight = tkeep.reshape(-1)[None, :, None]
    wanted = targets.reshape(asked, groups, local).transpose(1, 0, 2).astype(F32)
    diff = pred - wanted
    loss = jnp.sum(weight * diff * diff)
    grad_pred = (2.0 * weight * diff / total).astype(BF)
    g_head = dots("nd,gnk->gdk", head_in, grad_pred)
    grad_out, g_final = norm_back(
        norm_f, scale_f, final, dots("gnk,gdk->nd", grad_pred, w_head)
    )
    grad_mid, grad_mixed, g_o, g_up, g_down, g_second = rest_backward(
        grad_out, rest, mixed, w_o, w_up, w_down, second
    )
    gm = grad_mixed.reshape(shape_b)
    grad_probs = jnp.concatenate(
        [dots("gbnhs,gmhs->ghbnm", gm, v_c), dots("gbnhs,gbmhs->ghbnm", gm, v_t)], -1
    )
    grad_scores = (
        probs32 * (grad_probs - jnp.sum(grad_probs * probs32, -1, keepdims=True))
    ).astype(BF)
    ds_c, ds_t = (grad_scores[..., :nctx], grad_scores[..., nctx:])
    p_c, p_t = (probs[..., :nctx], probs[..., nctx:])
    root = size**-0.5
    grad_q = (
        (dots("ghbnm,gmhs->gbnhs", ds_c, k_c) + dots("ghbnm,gbmhs->gbnhs", ds_t, k_t)) * root
    ).astype(BF)
    grad_k_t = (dots("ghbnm,gbnhs->gbmhs", ds_t, q_b) * root).astype(BF)
    grad_v_t = dots("ghbnm,gbnhs->gbmhs", p_t, gm).astype(BF)
    grad_k_c = jnp.sum(
        (dots("ghbnm,gbnhs->gbmhs", ds_c, q_b) * root).astype(BF).astype(F32), 1
    )
    grad_v_c = jnp.sum(dots("ghbnm,gbnhs->gbmhs", p_c, gm).astype(BF).astype(F32), 1)
    kv_c = jnp.concatenate([merge_heads(grad_k_c), merge_heads(grad_v_c)], 2)
    high = kv_c.astype(BF)
    low = (kv_c - high.astype(F32)).astype(BF)
    flat = (groups, asked, plocal)
    t_rows = jnp.concatenate(
        [grad_q.reshape(flat), grad_k_t.reshape(flat), grad_v_t.reshape(flat)], 2
    )
    a_c, a_t = (mixer_in[:nctx], mixer_in[nctx:])
    g_q = dots("nd,gnk->gdk", a_t, t_rows[:, :, :plocal])
    g_kv = dots(
        "nd,gnk->gdk",
        jnp.concatenate([a_c, a_c, a_t], 0),
        jnp.concatenate([high, low, t_rows[:, :, plocal:]], 1),
    )
    w_kv = bank[:, :, plocal : 3 * plocal]
    grad_a = jnp.concatenate(
        [
            dots("gnk,gdk->nd", high, w_kv) + dots("gnk,gdk->nd", low, w_kv),
            dots("gnk,gdk->nd", t_rows, w_qkv),
        ],
        0,
    )
    grad_in, g_first = norm_back(norm1, scale1, first, grad_a)
    g_token = jnp.sum(grad_in[nctx:] + grad_mid, 0)
    grad_entry = grad_in[:nctx].astype(BF)
    g_entry = dots("nd,gnk->gdk", grad_entry, spread)
    grad_context = dots("nd,gdk->gnk", grad_entry, w_entry).transpose(1, 0, 2).reshape(nctx, -1)
    g_bank = jnp.concatenate([g_q, g_kv, g_o, g_up, g_down, g_head, g_entry], 2)
    return (grad_context, loss, g_bank, (g_first, g_second, g_final, g_token))


def per_device(
    pixels,
    context_slots,
    context_count,
    target_slots,
    target_count,
    encoder_in,
    encoder_out,
    predictor_in,
    predictor_out,
    vectors,
    first_encoder_in,
    first_encoder_out,
    first_predictor_in,
    first_predictor_out,
    first_vectors,
    second_encoder_in,
    second_encoder_out,
    second_predictor_in,
    second_predictor_out,
    second_vectors,
    target_encoder_in,
    target_encoder_out,
    target_vectors,
):
    groups = lax.axis_size("mp")
    owners = lax.axis_size("role") * lax.axis_size("dp")
    width = encoder_in.shape[0] * owners
    pwidth = predictor_in.shape[0] * owners
    local, plocal = (width // groups, pwidth // groups)
    pixel = pixels.shape[2]
    hidden = encoder_in.shape[1] - 3 * local
    phidden = predictor_in.shape[1] - 3 * plocal - local
    patches = pixels.shape[1]
    image = lax.axis_index("role") * groups + lax.axis_index("mp")

    def gather(packed):
        whole = lax.all_gather(packed.astype(BF), EVERY, axis=0, tiled=True)
        return whole.reshape(groups, -1, packed.shape[1])

    bank = gather(pack_encoder(encoder_in, encoder_out, local, pixel))
    pbank = gather(pack_predictor(predictor_in, predictor_out, local, plocal, phidden))
    tbank = gather(pack_encoder(target_encoder_in, target_encoder_out, local, pixel))
    both = lax.all_gather(
        jnp.stack([vectors, target_vectors]).astype(BF), ("role", "dp", "mp"), axis=0
    )
    s_vec = both[:, 0].reshape(-1).astype(F32)
    t_vec = both[:, 1].reshape(-1).astype(F32)
    target_total = lax.psum(jnp.sum(target_count).astype(F32), "dp")

    half = lax.dynamic_slice_in_dim(pixels, lax.axis_index("role") * groups, groups, 0)
    pix = lax.all_to_all(half, "mp", 0, 0, tiled=True)
    slots = lax.dynamic_index_in_dim(context_slots, image, 0, keepdims=False)
    count = lax.dynamic_index_in_dim(context_count, image, 0, keepdims=False)
    tslots = lax.dynamic_index_in_dim(target_slots, image, 0, keepdims=False)
    tcount = lax.dynamic_index_in_dim(target_count, image, 0, keepdims=False)
    nctx = slots.shape[0]
    blocks, tlen = tslots.shape

    patch = jnp.arange(patches)
    hits = slots[:, None] == patch[None, :]
    member = jnp.any(hits, 0)
    order = jnp.where(
        member,
        jnp.sum(jnp.where(hits, jnp.arange(nctx)[:, None], 0), 0),
        nctx + jnp.cumsum(1 - member.astype(jnp.int32)) - 1,
    )
    shuffle = order[None, :] == patch[:, None]
    places = jnp.sum(jnp.where(shuffle, patch[None, :], 0), 1)
    ckeep = (jnp.arange(nctx) < count).astype(F32)
    keep = (patch < count).astype(F32)
    tkeep = (jnp.arange(tlen)[None, :] < tcount[:, None]).astype(F32)

    table = sincos(width)
    sizes = (local, hidden, pixel)
    t_out, _ = encoder_forward(
        pix, table, jnp.ones_like(keep), tbank, (t_vec[:width], t_vec[width : 2 * width]),
        sizes, patches,
    )
    t_norm = layer_stats(t_out)[0].astype(BF)
    t_hot = (tslots.reshape(-1)[:, None] == patch[None, :]).astype(BF)
    targets = jnp.dot(t_hot, t_norm, preferred_element_type=F32).astype(BF)

    mixed_pix = dots("jp,gpk->gjk", shuffle.astype(BF), pix).astype(BF)
    enc_gains = (s_vec[:width], s_vec[width : 2 * width])
    latent, enc_saved = encoder_forward(
        mixed_pix, pick(table, places), keep, bank, enc_gains, sizes, nctx
    )
    pv = s_vec[2 * width :]
    pgains = (pv[:pwidth], pv[pwidth : 2 * pwidth], pv[2 * pwidth : 3 * pwidth], pv[3 * pwidth :])
    grad_context, loss, g_pbank, p_small = predictor(
        latent.astype(BF), targets, sincos(pwidth), slots, tslots, ckeep, tkeep, target_total,
        pbank, pgains, (local, plocal, phidden),
    )
    g_bank, g_first, g_second = encoder_backward(
        grad_context, enc_saved, mixed_pix, bank, enc_gains, sizes
    )
    g_vec = jnp.concatenate([g_first, g_second, *p_small])

    def scatter(grads):
        flat = grads.reshape(-1, grads.shape[-1])
        return lax.psum_scatter(flat, EVERY, scatter_dimension=0, tiled=True)

    r_pin, r_pout = unpack_predictor(scatter(g_pbank), local, plocal, phidden)
    r_in, r_out = unpack_encoder(scatter(g_bank), local, hidden, pixel)
    r_vec = lax.psum_scatter(g_vec, ("role", "dp", "mp"), scatter_dimension=0, tiled=True)
    squares = sum(jnp.sum(g * g) for g in (r_in, r_out, r_pin, r_pout, r_vec))
    squares, loss_total = lax.psum((squares, loss), ("role", "dp", "mp"))
    grad_norm = jnp.sqrt(squares)
    scale = jnp.minimum(1.0, CLIP / (grad_norm + 1e-06))
    new_in, m_in, v_in = adamw(
        encoder_in, r_in, first_encoder_in, second_encoder_in, scale, RATE_MATRIX, DECAY
    )
    new_out, m_out, v_out = adamw(
        encoder_out, r_out, first_encoder_out, second_encoder_out, scale, RATE_MATRIX, DECAY
    )
    new_pin, m_pin, v_pin = adamw(
        predictor_in, r_pin, first_predictor_in, second_predictor_in, scale, RATE_MATRIX, DECAY
    )
    new_pout, m_pout, v_pout = adamw(
        predictor_out, r_pout, first_predictor_out, second_predictor_out, scale, RATE_MATRIX, DECAY
    )
    new_vec, m_vec, v_vec = adamw(
        vectors, r_vec, first_vectors, second_vectors, scale, RATE_VECTOR, 0.0
    )
    ema_in = MOMENTUM_EMA * target_encoder_in + (1.0 - MOMENTUM_EMA) * new_in
    ema_out = MOMENTUM_EMA * target_encoder_out + (1.0 - MOMENTUM_EMA) * new_out
    ema_vec = MOMENTUM_EMA * target_vectors + (1.0 - MOMENTUM_EMA) * new_vec
    return (
        new_in, new_out, new_pin, new_pout, new_vec,
        m_in, m_out, m_pin, m_pout, m_vec,
        v_in, v_out, v_pin, v_pout, v_vec,
        ema_in, ema_out, ema_vec,
        loss_total, target_total, grad_norm,
    )


def solution(mesh):
    bank_in, bank_out, small = (
        P(("role", "dp"), "mp"),
        P("mp", ("role", "dp")),
        P(("role", "dp", "mp")),
    )
    five = (bank_in, bank_out, bank_in, bank_out, small)
    three = (bank_in, bank_out, small)
    return jax.shard_map(
        per_device,
        mesh=mesh,
        in_specs=(
            P("dp", None, "mp"),
            P("dp", None),
            P("dp"),
            P("dp", None, None),
            P("dp", None),
        )
        + five * 3
        + three,
        out_specs=five * 3 + three + (P(), P(), P()),
        check_vma=False,
    )
```

time: 2390 us -> 935 us (0.39)
  waiting for transfers between devices: 1510 us -> 459 us
  blocking collectives: 289 us -> 158 us
  matrix products: 251 us -> 137 us
  local copies, waits for them, and re-layouts: 180 us -> 90.3 us
  other arithmetic: 129 us -> 49.8 us
    unnamed x39 -> x5, waiting for transfers between devices: 364 us -> 0.08 us
    all_gather x15 -> x3, waiting for transfers between devices: 499 us -> 165 us  [gather(): whole = lax.all_gather(packed.astype(BF), EVERY, axis=0, tiled=True)]
    reduce_scatter x7 -> x2, waiting for transfers between devices: 586 us -> 294 us  [scatter(): return lax.psum_scatter(flat, EVERY, scatter_dimension=0, tiled=True)]
    dot_general x44 -> x62, matrix products: 251 us -> 133 us  [the longest x58 131 us: dots(): return jnp.einsum(spec, left, right, preferred_element_type=F32)]
    psum x3 -> x2, blocking collectives: 150 us -> 53 us  [the longest x1 40.4 us: per_device(): squares, loss_total = lax.psum((squares, loss), ('role', 'dp', 'mp'))]
    psum x1 -> x0, waiting for transfers between devices: 57.3 us -> none  [context_total(): return lax.psum(terms, 'mp')]
    unnamed x2 -> x1, blocking collectives: 84.6 us -> 39 us
    gather x4 -> x0, local copies, waits for them, and re-layouts: 44.6 us -> none  [the longest x1 26.2 us: per_device(): full[image_ids[:, None, None], target_slots]]
  transfers between devices with their start and end apart: 32 -> 6, of which waited for: 29 -> 5; matrix products, arithmetic and copies ran while one was open for 5% -> 14% of each run, Pallas kernels for 0% -> 0%
where the time goes in v1:
time: 935 us; the launch traced here: 922 us
  waiting for transfers between devices  459 us (49%)
  blocking collectives  158 us (17%)
  matrix products  137 us (15%)
  local copies, waits for them, and re-layouts  90.3 us (10%)
  other arithmetic  49.8 us (5%)
  between operations  22.2 us (2%)
    reduce_scatter x2, waiting for transfers between devices, scatter(): return lax.psum_scatter(flat, EVERY, scatter_dimension=0, tiled=True)  294 us
    all_gather x3, waiting for transfers between devices, gather(): whole = lax.all_gather(packed.astype(BF), EVERY, axis=0, tiled=True)  165 us
    dot_general x58, matrix products, dots(): return jnp.einsum(spec, left, right, preferred_element_type=F32)  131 us
    all_gather x1, blocking collectives, per_device(): lax.all_gather(jnp.stack([vectors, target_vectors]).astype(BF), ('role',...  65.6 us
    psum x1, blocking collectives, per_device(): squares, loss_total = lax.psum((squares, loss), ('role', 'dp', 'mp'))  40.4 us
    unnamed x1, blocking collectives  39 us
    concatenate x1, local copies, waits for them, and re-layouts, encoder_backward(): jnp.concatenate([g_qkv, g_o, g_up, g_down, g_emb], 2)  30.7 us
    sub x1, other arithmetic, predictor(): grad_probs - jnp.sum(grad_probs * probs32, -1, keepdims=True)  20.7 us
  transfers between devices with their start and end apart: 6, of which 5 were waited for; matrix products, arithmetic and copies ran while one was open for 14% of the time, Pallas kernels for 0%

profile of v1, /device:TPU:0, one launch (start us, length us, event | category | flops | bytes accessed | tf_op | source)
XLA Modules:
  0.0 922.1 jit_solution(3802585140587439263)
XLA Ops:
  15.4 5.2 all-to-all-start
  20.6 12.6 %psum.21 = f32[]{:T(128)} all-reduce(f32[]{:T(128)S(6)} %convert_element_type.300), channel_id=1, replica_groups=mesh['role'=2,'dp'=4,'mp'=4] {'dp'}, use_global_device_ids=true, to_apply=%region_29.30 | all-reduce | flops 1 | bytes 8 | tf_op jit(solution)/shard_map/psum | solution.py:393
  38.0 65.6 %all_gather.14 = bf16[32,2,96]{2,1,0:T(2,128)(2,1)S(1)} all-gather(bf16[1,2,96]{2,1,0:T(2,128)(2,1)S(1)} %pad_maximum_fusion.8), channel_id=1, replica_groups=mesh['role'=2,'dp'=4,'mp'=4] {'role','dp','mp'}, dimensions={0}, use_global_device_ids=true | all-gather | bytes 12672 | tf_op jit(solution)/shard_map/all_gather | solution.py:388
  108.0 17.6 %all-gather.4.cloned.1.call-done = bf16[3072,2496]{1,0:T(8,128)(2,1)} async-done(((bf16[96,2496]{1,0:T(8,128)(2,1)}), bf16[3072,2496]{1,0:T(8,128)(2,1)}) %all-gather.4.cloned.1.call-update) | async-done | bytes 15335440 | tf_op jit(solution)/shard_map/all_gather | solution.py:382
  128.6 3.1 fusion.85
  135.8 3.0 fusion.357
  139.1 3.3 fusion.13
  142.5 5.5 fusion.160
  149.2 41.6 %all-gather.6.cloned.1.call-done = bf16[1536,1536]{1,0:T(8,128)(2,1)} async-done(((bf16[48,1536]{1,0:T(8,128)(2,1)}), bf16[1536,1536]{1,0:T(8,128)(2,1)}) %all-gather.6.cloned.1.call-update) | async-done | bytes 4718608 | tf_op jit(solution)/shard_map/all_gather | solution.py:382
  197.0 106.1 %all-gather.8.cloned.1.call-done = bf16[3072,2496]{1,0:T(8,128)(2,1)} async-done(((bf16[96,2496]{1,0:T(8,128)(2,1)}), bf16[3072,2496]{1,0:T(8,128)(2,1)}) %all-gather.8.cloned.1.call-update) | async-done | bytes 15335440 | tf_op jit(solution)/shard_map/all_gather | solution.py:382
  305.6 3.4 fusion.82
  314.4 2.9 fusion.362
  317.5 6.6 fusion.363
  345.3 2.6 fusion.369
  359.9 2.8 convert_reduce_fusion
  365.1 20.7 %multiply_convert_fusion = bf16[4,3,4,64,224]{4,3,2,1,0:T(8,128)(2,1)S(1)} fusion(f32[4,3,4,64,64]{4,3,2,1,0:T(8,128)S(1)} %fusion.222, f32[4,3,4,64,160]{4,3,2,1,0:T(8,128)S(1)} %fusion.224, f32[4,3,4,64]{3,2,1,0:T(4,128)S(1)} %copy-done.98, f32[4,3,4,64]{3,2,1,0:T(4,128)S(1)} %copy-done.92, f32[4,3,4,64,64]{4,3,2,1,0:T(8,128)S(1)} %copy-done.3, ...), kind=kOutput, calls=%fused_computation.27 | output fusion | flops 8260831 | bytes 6905856 | tf_op jit(solution)/shard_map/sub | solution.py:300
  409.4 2.9 fusion.72
  421.6 9.6 %copy.275 = f32[4,384,1536]{2,1,0:T(8,128)} copy(f32[4,384,1536]{1,2,0:T(8,128)} %fusion.76) | data formatting | bytes 18874368 | tf_op jit(solution)/shard_map/concatenate | solution.py:341
  434.0 4.7 fusion.34
  438.7 4.8 multiply_reduce_fusion.15
  443.8 2.6 fusion.163
  450.4 2.9 multiply_reduce_fusion.2
  461.7 4.4 multiply_reduce_fusion.6
  466.2 4.6 bitcast_dynamic-update-slice_fusion.2
  472.7 5.1 bitcast_dynamic-update-slice_fusion.1
  477.8 5.4 bitcast_dynamic-update-slice_fusion
  485.4 30.7 %copy.272 = f32[4,768,2496]{2,1,0:T(8,128)} copy(f32[4,768,2496]{1,2,0:T(8,128)} %bitcast_dynamic-update-slice_fusion.5) | data formatting | bytes 61341696 | tf_op jit(solution)/shard_map/concatenate | solution.py:233
  517.3 39.0 %all-reduce.3 = f32[3072]{0:T(1024)S(1)} all-reduce(f32[3072]{0:T(1024)S(1)} %constant_dynamic-update-slice_fusion.4), channel_id=4, replica_groups=mesh['role'=2,'dp'=4,'mp'=4] {'role','dp','mp'}, use_global_device_ids=true, to_apply=%region_56.57.clone | all-reduce | flops 3072 | bytes 24576
  557.0 8.7 reduce-scatter.5.cloned.1.call-done
  570.6 285.3 %reduce-scatter.3.cloned.1.call-done = f32[96,2496]{1,0:T(8,128)} async-done(((f32[3072,2496]{1,0:T(8,128)}), f32[96,2496]{1,0:T(8,128)}) %reduce-scatter.3.cloned.1.call-update) | async-done | bytes 958480 | tf_op jit(solution)/shard_map/reduce_scatter | solution.py:446
  863.9 40.4 %all-reduce.4 = (f32[]{:T(128)}, f32[]{:T(128)}) all-reduce(f32[]{:T(128)S(6)} %add.372, f32[]{:T(128)} %get-tuple-element.115), channel_id=1, replica_groups=mesh['role'=2,'dp'=4,'mp'=4] {'role','dp','mp'}, use_global_device_ids=true, to_apply=%region_58.59 | all-reduce | flops 2 | bytes 16 | tf_op jit(solution)/shard_map/psum | solution.py:452
  909.6 2.6 multiply_add_fusion.7
  (514 shorter events, 143.7 us)
Async XLA Ops:
  7.2 118.4 %all-gather.4.cloned.1.call-start = ((), (), s32[]{:S(2)}) async-start(), calls=%async_computation.3 | async-start | bytes 16220160 | tf_op jit(solution)/shard_map/all_gather | solution.py:382
  10.7 180.1 %all-gather.6.cloned.1.call-start = ((), (), s32[]{:S(2)}) async-start(), calls=%async_computation.4 | async-start | bytes 4866048 | tf_op jit(solution)/shard_map/all_gather | solution.py:382
  12.0 291.2 %all-gather.8.cloned.1.call-start = ((), (), s32[]{:S(2)}) async-start(), calls=%async_computation.5 | async-start | bytes 16220160 | tf_op jit(solution)/shard_map/all_gather | solution.py:382
  12.2 21.1 %copy-start.137 = (s32[8]{0:T(128)S(1)}, s32[8]{0:T(128)}, u32[]{:S(2)}) copy-start(s32[8]{0:T(128)} %param.27) | copy-start | bytes 100
  12.3 25.7 %copy-start.133 = (f32[96]{0:T(128)S(1)}, f32[96]{0:T(128)}, u32[]{:S(2)}) copy-start(f32[96]{0:T(128)} %param.34) | copy-start | bytes 1156
  12.3 25.7 %copy-start.131 = (f32[96]{0:T(128)S(1)}, f32[96]{0:T(128)}, u32[]{:S(2)}) copy-start(f32[96]{0:T(128)} %param.47) | copy-start | bytes 1156
  12.3 95.0 %copy-start.67 = (f32[196,384]{1,0:T(8,128)S(1)}, f32[196,384]{1,0:T(8,128)}, u32[]{:S(2)}) copy-start(f32[196,384]{1,0:T(8,128)} %constant.95.clone) | copy-start | bytes 903172
  15.4 92.3 %all-to-all-start = ((bf16[4,196,192]{1,2,0:T(8,128)(2,1)}), bf16[4,196,192]{1,2,0:T(8,128)(2,1)S(1)}, u32[]{:S(2)}, u32[]{:S(2)}) async-start(bf16[4,196,192]{1,2,0:T(8,128)(2,1)} %constant_dynamic-slice_fusion.2), calls=%async_computation | async-start | bytes 786432 | tf_op jit(solution)/shard_map/all_to_all | solution.py:396
  20.6 545.1 %reduce-scatter.5.cloned.1.call-start = ((), (), s32[]{:S(2)}) async-start(), calls=%async_computation.7 | async-start | bytes 9732096 | tf_op jit(solution)/shard_map/reduce_scatter | solution.py:446
  104.8 23.8 %copy-start.111 = (f32[768]{0:T(1024)}, f32[768]{0:T(1024)S(1)}, u32[]{:S(2)}) copy-start(f32[768]{0:T(1024)S(1)} %slice.305) | copy-start | bytes 9220
  105.6 29.0 %copy-start.138 = (f32[196]{0:T(256)}, f32[196]{0:T(256)S(1)}, u32[]{:S(2)}) copy-start(f32[196]{0:T(256)S(1)} %fusion.302) | copy-start | bytes 2356
  107.3 20.5 %copy-start.42 = (f32[196,768]{1,0:T(8,128)S(1)}, f32[196,768]{1,0:T(8,128)}, u32[]{:S(2)}) copy-start(f32[196,768]{1,0:T(8,128)} %constant.94.clone) | copy-start | bytes 1806340
  108.0 20.3 %copy-start.52 = (bf16[4,196,192]{1,2,0:T(8,128)(2,1)}, bf16[4,196,192]{1,2,0:T(8,128)(2,1)S(1)}, u32[]{:S(2)}) copy-start(bf16[4,196,192]{1,2,0:T(8,128)(2,1)S(1)} %fusion.158) | copy-start | bytes 903172
  142.5 50.3 %copy-start.17 = (f32[4,768,160]{1,2,0:T(8,128)}, f32[4,768,160]{1,2,0:T(8,128)S(1)}, u32[]{:S(2)}) copy-start(f32[4,768,160]{1,2,0:T(8,128)S(1)} %fusion.13) | copy-start | bytes 5898244
  147.9 44.5 %copy-start.68 = (f32[196,384]{1,0:T(8,128)S(1)}, f32[196,384]{1,0:T(8,128)}, u32[]{:S(2)}) copy-start(f32[196,384]{1,0:T(8,128)} %constant.95.clone) | copy-start | bytes 903172
  149.2 44.5 %copy-start.61 = (bf16[160,4,192]{2,1,0:T(4,128)(2,1)}, bf16[160,4,192]{2,1,0:T(4,128)(2,1)S(1)}, u32[]{:S(2)}) copy-start(bf16[160,4,192]{2,1,0:T(4,128)(2,1)S(1)} %reshape.434) | copy-start | bytes 737284
  193.7 109.4 %copy-start.29 = (bf16[4,196,192]{1,2,0:T(8,128)(2,1)S(1)}, bf16[4,196,192]{1,2,0:T(8,128)(2,1)}, u32[]{:S(2)}) copy-start(bf16[4,196,192]{1,2,0:T(8,128)(2,1)} %copy-done.28) | copy-start | bytes 903172
  193.7 109.4 %copy-start.43 = (f32[196,768]{1,0:T(8,128)S(1)}, f32[196,768]{1,0:T(8,128)}, u32[]{:S(2)}) copy-start(f32[196,768]{1,0:T(8,128)} %constant.94.clone) | copy-start | bytes 1806340
  197.0 129.9 %copy-start.38 = (bf16[4,416,96]{1,2,0:T(8,128)(2,1)}, bf16[4,416,96]{1,2,0:T(8,128)(2,1)S(1)}, u32[]{:S(2)}) copy-start(bf16[4,416,96]{1,2,0:T(8,128)(2,1)S(1)} %get-tuple-element.65) | copy-start | bytes 958468
  197.0 131.0 %copy-start.39 = (bf16[4,416,96]{1,2,0:T(8,128)(2,1)}, bf16[4,416,96]{1,2,0:T(8,128)(2,1)S(1)}, u32[]{:S(2)}) copy-start(bf16[4,416,96]{1,2,0:T(8,128)(2,1)S(1)} %get-tuple-element.64) | copy-start | bytes 958468
  365.1 20.7 %copy-start.35 = (bf16[4,4,64,3,32]{2,1,4,3,0:T(4,128)(2,1)S(1)}, bf16[4,4,64,3,32]{2,1,4,3,0:T(4,128)(2,1)}, u32[]{:S(2)}) copy-start(bf16[4,4,64,3,32]{2,1,4,3,0:T(4,128)(2,1)} %reshape.437) | copy-start | bytes 589828
  431.2 424.7 %reduce-scatter.3.cloned.1.call-start = ((), (), s32[]{:S(2)}) async-start(), calls=%async_computation.6 | async-start | bytes 32440320 | tf_op jit(solution)/shard_map/reduce_scatter | solution.py:446
  570.6 334.4 %copy-start.132 = (f32[96]{0:T(128)S(1)}, f32[96]{0:T(128)}, u32[]{:S(2)}) copy-start(f32[96]{0:T(128)} %param.47) | copy-start | bytes 1156
  570.6 334.5 %copy-start.134 = (f32[96]{0:T(128)S(1)}, f32[96]{0:T(128)}, u32[]{:S(2)}) copy-start(f32[96]{0:T(128)} %param.34) | copy-start | bytes 1156
  570.6 334.5 %copy-start.135 = (f32[96]{0:T(128)S(1)}, f32[96]{0:T(128)}, u32[]{:S(2)}) copy-start(f32[96]{0:T(128)} %param.39) | copy-start | bytes 1156
  570.6 334.5 %copy-start.136 = (f32[96]{0:T(128)S(1)}, f32[96]{0:T(128)}, u32[]{:S(2)}) copy-start(f32[96]{0:T(128)} %param.44) | copy-start | bytes 1156
  570.6 335.1 %copy-start.80 = (f32[672,48]{0,1:T(8,128)S(1)}, f32[672,48]{0,1:T(8,128)}, u32[]{:S(2)}) copy-start(f32[672,48]{0,1:T(8,128)} %param.33) | copy-start | bytes 387076
  858.1 49.6 %copy-start.78 = (f32[48,864]{1,0:T(8,128)S(1)}, f32[48,864]{1,0:T(8,128)}, u32[]{:S(2)}) copy-start(f32[48,864]{1,0:T(8,128)} %param.32) | copy-start | bytes 497668
  858.1 49.6 %copy-start.96 = (f32[48,864]{1,0:T(8,128)S(1)}, f32[48,864]{1,0:T(8,128)}, u32[]{:S(2)}) copy-start(f32[48,864]{1,0:T(8,128)} %param.37) | copy-start | bytes 497668
  858.2 51.3 %copy-start.48 = (f32[1152,96]{0,1:T(8,128)S(1)}, f32[1152,96]{0,1:T(8,128)}, u32[]{:S(2)}) copy-start(f32[1152,96]{0,1:T(8,128)} %param.31) | copy-start | bytes 1327108
  858.2 51.3 %copy-start.50 = (f32[1152,96]{0,1:T(8,128)S(1)}, f32[1152,96]{0,1:T(8,128)}, u32[]{:S(2)}) copy-start(f32[1152,96]{0,1:T(8,128)} %param.46) | copy-start | bytes 1327108
  858.2 51.3 %copy-start.83 = (f32[1152,96]{0,1:T(8,128)S(1)}, f32[1152,96]{0,1:T(8,128)}, u32[]{:S(2)}) copy-start(f32[1152,96]{0,1:T(8,128)} %param.36) | copy-start | bytes 1327108
  (117 other events, 400.8 us)
Sparse Core Ops, SparseCore 0:
  11.4 114.1 all-gather.3
  129.0 61.7 all-gather.5
  194.2 108.8 all-gather.7
  431.3 134.2 reduce-scatter.4
  573.0 282.8 reduce-scatter.2

commit v2 on v1

--- a/solution.py
+++ b/solution.py
@@ -1,7 +1,11 @@
+import functools
+
 import jax
 import jax.numpy as jnp
 import numpy as np
 from jax import lax
+from jax.experimental import pallas as pl
+from jax.experimental.pallas import tpu as pltpu
 from jax.sharding import PartitionSpec as P
 
 HEADS = 12
@@ -21,7 +25,7 @@
 
 BF = jnp.bfloat16
 F32 = jnp.float32
-EVERY = ("mp", "role", "dp")
+LANES = 128
 
 
 def dots(spec, left, right):
@@ -73,8 +77,9 @@
     )
 
 
-def pack_encoder(w_in, w_out, local, pixel):
+def pack_encoder(w_in, w_out, local, pixel, extras):
     turned = w_out.T
+    used = w_in.shape[1] + turned.shape[1] + len(extras)
     return jnp.concatenate(
         [
             w_in[:, : 3 * local],
@@ -82,9 +87,11 @@
             w_in[:, 3 * local :],
             turned[:, pixel + local :],
             turned[:, :pixel],
+            *[e[:, None] for e in extras],
+            jnp.zeros((w_in.shape[0], -used % (2 * LANES)), F32),
         ],
         1,
-    )
+    ).astype(BF)
 
 
 def unpack_encoder(packed, local, hidden, pixel):
@@ -93,7 +100,7 @@
     emb = down + hidden
     w_in = jnp.concatenate([packed[:, : 3 * local], packed[:, up:down]], 1)
     turned = jnp.concatenate(
-        [packed[:, emb:], packed[:, 3 * local : up], packed[:, down:emb]], 1
+        [packed[:, emb : emb + pixel], packed[:, 3 * local : up], packed[:, down:emb]], 1
     )
     return (w_in, turned.T)
 
@@ -110,7 +117,7 @@
             turned[:, :local],
         ],
         1,
-    )
+    ).astype(BF)
 
 
 def unpack_predictor(packed, local, plocal, phidden):
@@ -174,6 +181,515 @@
     return (grad_mid, grad_mixed, g_o, g_up, g_down, g_second)
 
 
+def shift_of(rank, by):
+    return jnp.bitwise_xor(rank, by)
+
+
+def greet(peers):
+    barrier = pltpu.get_barrier_semaphore()
+    for peer in peers:
+        pl.semaphore_signal(barrier, inc=1, device_id=peer, device_id_type=pl.DeviceIdType.MESH)
+    pl.semaphore_wait(barrier, len(peers))
+
+
+def gather_kernel(nz, count, *refs):
+    ins = refs[:count]
+    outs = refs[count : 2 * count]
+    (own_sem, zs, zr, xs, xr, ys, yr, rxs, rxr, rys, ryr, cs, cr) = refs[2 * count :]
+    r = lax.axis_index("role")
+    d = lax.axis_index("dp")
+    m = lax.axis_index("mp")
+    mx = shift_of(m, 1)
+    my = shift_of(m, 2)
+    base = r * nz
+    line_of = [{"dp": lax.rem(d + j, nz)} for j in range(1, nz)]
+    greet([{"role": 1 - r}, {"mp": mx}, {"mp": my}] + line_of)
+
+    def remote(src, dst, send, recv, where):
+        return pltpu.make_async_remote_copy(
+            src_ref=src, dst_ref=dst, send_sem=send, recv_sem=recv,
+            device_id=where, device_id_type=pl.DeviceIdType.MESH,
+        )
+
+    def line(k, piece, way, from_input=False):
+        out = outs[k]
+        src = ins[k] if from_input else out.at[m, base + piece]
+        return remote(
+            src, out.at[m, base + piece], zs.at[k, way, piece], zr.at[k, way, piece],
+            {"dp": d + 1 - 2 * way},
+        )
+
+    def across(k, piece, from_input=False):
+        out = outs[k]
+        src = ins[k] if from_input else out.at[m, base + piece]
+        dst = out.at[m, base + piece]
+        return (
+            remote(src, dst, xs.at[k, piece], xr.at[k, piece], {"mp": mx}),
+            remote(src, dst, ys.at[k, piece], yr.at[k, piece], {"mp": my}),
+        )
+
+    def arrived(k, piece):
+        out = outs[k]
+        return (
+            remote(out.at[mx, base + piece], out.at[mx, base + piece], xs.at[k, piece], xr.at[k, piece], {"mp": mx}),
+            remote(out.at[my, base + piece], out.at[my, base + piece], ys.at[k, piece], yr.at[k, piece], {"mp": my}),
+        )
+
+    def relay(k, piece):
+        out = outs[k]
+        half = out.shape[3] // 2
+        first = out.at[mx, base + piece, :, pl.ds(0, half)]
+        second = out.at[my, base + piece, :, pl.ds(half, half)]
+        return (
+            remote(first, first, rys.at[k, piece], ryr.at[k, piece], {"mp": my}),
+            remote(second, second, rxs.at[k, piece], rxr.at[k, piece], {"mp": mx}),
+        )
+
+    def diagonal(k, piece):
+        out = outs[k]
+        half = out.shape[3] // 2
+        far = shift_of(m, 3)
+        first = out.at[far, base + piece, :, pl.ds(0, half)]
+        second = out.at[far, base + piece, :, pl.ds(half, half)]
+        return (
+            remote(first, first, rys.at[k, piece], ryr.at[k, piece], {"mp": my}),
+            remote(second, second, rxs.at[k, piece], rxr.at[k, piece], {"mp": mx}),
+        )
+
+    def core(k, column, slot):
+        block = outs[k].at[column, pl.ds(base, nz)]
+        return remote(block, block, cs.at[k, slot], cr.at[k, slot], {"role": 1 - r})
+
+    def core_in(k, column, slot):
+        block = outs[k].at[column, pl.ds((1 - r) * nz, nz)]
+        return remote(block, block, cs.at[k, slot], cr.at[k, slot], {"role": 1 - r})
+
+    def owncopy(k):
+        return pltpu.make_async_copy(ins[k], outs[k].at[m, base + d], own_sem.at[k])
+
+    for k in range(count):
+        @pl.when(d < nz - 1)
+        def _():
+            line(k, d, 0, True).start()
+
+        @pl.when(d > 0)
+        def _():
+            line(k, d, 1, True).start()
+
+        for copy in across(k, d, True):
+            copy.start()
+        owncopy(k).start()
+
+    for k in range(count):
+        def pass_on(piece):
+            for copy in arrived(k, piece):
+                copy.wait_recv()
+            for copy in relay(k, piece):
+                copy.start()
+
+        def step(t, carry):
+            left = d - 1 - t
+            right = d + 1 + t
+
+            @pl.when(left >= 0)
+            def _():
+                line(k, left, 0).wait_recv()
+
+                @pl.when(d < nz - 1)
+                def _():
+                    line(k, left, 0).start()
+
+                for copy in across(k, left):
+                    copy.start()
+
+            @pl.when(right < nz)
+            def _():
+                line(k, right, 1).wait_recv()
+
+                @pl.when(d > 0)
+                def _():
+                    line(k, right, 1).start()
+
+                for copy in across(k, right):
+                    copy.start()
+
+            @pl.when(t == 0)
+            def _():
+                pass_on(d)
+
+            @pl.when(jnp.logical_and(t > 0, left + 1 >= 0))
+            def _():
+                pass_on(left + 1)
+
+            @pl.when(jnp.logical_and(t > 0, right - 1 < nz))
+            def _():
+                pass_on(right - 1)
+
+            return carry
+
+        lax.fori_loop(0, nz - 1, step, 0)
+        if nz == 1:
+            pass_on(d)
+        else:
+            @pl.when(d == nz - 1)
+            def _():
+                pass_on(0)
+
+            @pl.when(d == 0)
+            def _():
+                pass_on(nz - 1)
+
+        owncopy(k).wait()
+        core(k, m, 0).start()
+        core(k, mx, 1).start()
+        core(k, my, 2).start()
+
+    for k in range(count):
+        def take(piece, carry):
+            for copy in diagonal(k, piece):
+                copy.wait_recv()
+            return carry
+
+        lax.fori_loop(0, nz, take, 0)
+        core(k, shift_of(m, 3), 3).start()
+    for k in range(count):
+        columns = (m, mx, my, shift_of(m, 3))
+        for slot, column in enumerate(columns):
+            core_in(k, column, slot).wait_recv()
+            core(k, column, slot).wait_send()
+
+        def done(piece, carry):
+            for copy in across(k, piece):
+                copy.wait_send()
+            for copy in relay(k, piece):
+                copy.wait_send()
+
+            @pl.when(jnp.logical_and(piece <= d, d < nz - 1))
+            def _():
+                line(k, piece, 0).wait_send()
+
+            @pl.when(jnp.logical_and(piece >= d, d > 0))
+            def _():
+                line(k, piece, 1).wait_send()
+
+            return carry
+
+        lax.fori_loop(0, nz, done, 0)
+
+
+def gather_all(packs):
+    nz = lax.axis_size("dp")
+    groups = lax.axis_size("mp")
+    count = len(packs)
+    dma = pltpu.SemaphoreType.DMA
+    piece = dma((count, nz))
+    return pl.pallas_call(
+        functools.partial(gather_kernel, nz, count),
+        out_shape=[
+            jax.ShapeDtypeStruct((groups, lax.axis_size("role") * nz, *p.shape), p.dtype)
+            for p in packs
+        ],
+        in_specs=[pl.BlockSpec(memory_space=pl.ANY)] * count,
+        out_specs=[pl.BlockSpec(memory_space=pl.ANY)] * count,
+        scratch_shapes=[dma((count,)), dma((count, 2, nz)), dma((count, 2, nz))]
+        + [piece] * 8
+        + [dma((count, 4)), dma((count, 4))],
+        compiler_params=pltpu.CompilerParams(collective_id=1, has_side_effects=True),
+    )(*packs)
+
+
+def reduce_kernel(nz, count, stats_in, *refs):
+    ins = refs[:count]
+    outs = refs[count : 2 * count]
+    stats_out = refs[2 * count]
+    rest = refs[2 * count + 1 :]
+    accs = rest[:count]
+    loads = rest[count : 2 * count]
+    sends1 = rest[2 * count : 3 * count]
+    recvs1 = rest[3 * count : 4 * count]
+    sends2 = rest[4 * count : 5 * count]
+    recvs2 = rest[5 * count : 6 * count]
+    lines = rest[6 * count : 7 * count]
+    (near, near_in, far_in, ld, cs, cr, s1s, s1r, s2s, s2r, zs, zr, ns, nr, fs, fr) = rest[
+        7 * count :
+    ]
+    r = lax.axis_index("role")
+    d = lax.axis_index("dp")
+    m = lax.axis_index("mp")
+    groups = 4
+    mx = shift_of(m, 1)
+    my = shift_of(m, 2)
+    mf = shift_of(m, 3)
+    columns = (mf, mx, my, m)
+    group = [
+        {"role": role, "mp": shift_of(m, by)}
+        for role in (r, 1 - r)
+        for by in range(groups)
+    ][1:]
+    far = [{"dp": lax.rem(d + j, nz)} for j in range(1, nz)]
+    greet(group + far)
+
+    def remote(src, dst, send, recv, where):
+        return pltpu.make_async_remote_copy(
+            src_ref=src, dst_ref=dst, send_sem=send, recv_sem=recv,
+            device_id=where, device_id_type=pl.DeviceIdType.MESH,
+        )
+
+    def core(k, j):
+        return remote(
+            ins[k].at[columns[j], pl.ds((1 - r) * nz, nz)], accs[k].at[columns[j]],
+            cs.at[k, j], cr.at[k, j], {"role": 1 - r},
+        )
+
+    def load(k, j):
+        return pltpu.make_async_copy(
+            ins[k].at[columns[j], pl.ds(r * nz, nz)], loads[k].at[j % 2], ld.at[k, j % 2]
+        )
+
+    def first(k, piece):
+        half = ins[k].shape[3] // 2
+        low, high = (pl.ds(0, half), pl.ds(half, half))
+        return (
+            remote(sends1[k].at[piece, :, low], recvs1[k].at[piece, :, low],
+                   s1s.at[k, 0, piece], s1r.at[k, 0, piece], {"mp": my}),
+            remote(sends1[k].at[piece, :, high], recvs1[k].at[piece, :, high],
+                   s1s.at[k, 1, piece], s1r.at[k, 1, piece], {"mp": mx}),
+        )
+
+    def second(k, piece):
+        return (
+            remote(sends2[k].at[0, piece], recvs2[k].at[0, piece],
+                   s2s.at[k, 0, piece], s2r.at[k, 0, piece], {"mp": mx}),
+            remote(sends2[k].at[1, piece], recvs2[k].at[1, piece],
+                   s2s.at[k, 1, piece], s2r.at[k, 1, piece], {"mp": my}),
+        )
+
+    def right(k, piece):
+        return remote(accs[k].at[m, piece], lines[k].at[piece], zs.at[k, piece],
+                      zr.at[k, piece], {"dp": d + 1})
+
+    def left(k, piece):
+        slot = jnp.where(piece == d - 1, nz, piece)
+        return remote(accs[k].at[m, piece], lines[k].at[slot], zs.at[k, piece],
+                      zr.at[k, slot], {"dp": d - 1})
+
+    def line_in(k, slot):
+        return pltpu.make_async_remote_copy(
+            src_ref=lines[k].at[slot], dst_ref=lines[k].at[slot], send_sem=zs.at[k, 0],
+            recv_sem=zr.at[k, slot], device_id={"role": 1 - r},
+            device_id_type=pl.DeviceIdType.MESH,
+        )
+
+    def each(body):
+        def step(t, carry):
+            off = nz - 1 - t
+
+            @pl.when(d + off < nz)
+            def _():
+                body(d + off)
+
+            @pl.when(d - off >= 0)
+            def _():
+                body(d - off)
+
+            return carry
+
+        lax.fori_loop(0, nz - 1, step, 0)
+        body(d)
+
+    for k in range(count):
+        core(k, 0).start()
+        load(k, 0).start()
+        load(k, 1).start()
+    for j in range(1, groups):
+        for k in range(count):
+            core(k, j).start()
+
+    def combine(k, j):
+        core(k, j).wait_recv()
+        load(k, j).wait()
+
+    for k in range(count):
+        combine(k, 0)
+
+        def send_far(piece):
+            sends1[k][piece] = (accs[k][mf, piece] + loads[k][0, piece]).astype(sends1[k].dtype)
+            for copy in first(k, piece):
+                copy.start()
+
+        each(send_far)
+        load(k, 2).start()
+    for k in range(count):
+        half = ins[k].shape[3] // 2
+        combine(k, 1)
+
+        def add_x(piece, carry):
+            accs[k][mx, piece] += loads[k][1, piece]
+            return carry
+
+        lax.fori_loop(0, nz, add_x, 0)
+        load(k, 3).start()
+        combine(k, 2)
+
+        def send_near(piece):
+            for copy in first(k, piece):
+                copy.wait_recv()
+            relayed = recvs1[k][piece].astype(jnp.float32)
+            lane = lax.broadcasted_iota(jnp.int32, relayed.shape, 1)
+            sends2[k][0, piece] = (
+                accs[k][mx, piece] + jnp.where(lane < half, relayed, 0.0)
+            ).astype(sends2[k].dtype)
+            sends2[k][1, piece] = (
+                accs[k][my, piece] + loads[k][0, piece] + jnp.where(lane < half, 0.0, relayed)
+            ).astype(sends2[k].dtype)
+            for copy in second(k, piece):
+                copy.start()
+
+        each(send_near)
+    squares = jnp.zeros((1, 1), jnp.float32)
+    for k in range(count):
+        combine(k, 3)
+
+        def finish(piece):
+            for copy in second(k, piece):
+                copy.wait_recv()
+            accs[k][m, piece] += (
+                loads[k][1, piece]
+                + recvs2[k][0, piece].astype(jnp.float32)
+                + recvs2[k][1, piece].astype(jnp.float32)
+            )
+
+            @pl.when(piece > d)
+            def _():
+                @pl.when(d > 0)
+                def _():
+                    line_in(k, piece).wait_recv()
+                    accs[k][m, piece] += lines[k][piece]
+
+                right(k, piece).start()
+
+            @pl.when(piece < d)
+            def _():
+                @pl.when(d < nz - 1)
+                def _():
+                    line_in(k, piece).wait_recv()
+                    accs[k][m, piece] += lines[k][piece]
+
+                left(k, piece).start()
+
+        each(finish)
+    for k in range(count):
+        outs[k][...] = accs[k][m, d]
+
+        @pl.when(d > 0)
+        def _():
+            line_in(k, d).wait_recv()
+            outs[k][...] += lines[k][d]
+
+        @pl.when(d < nz - 1)
+        def _():
+            line_in(k, nz).wait_recv()
+            outs[k][...] += lines[k][nz]
+
+        total = outs[k][...]
+        squares += jnp.sum(total * total, keepdims=True)
+
+    mine = r * groups + m
+    row = lax.broadcasted_iota(jnp.int32, (8, 128), 0)
+    near[...] = jnp.where(row == 0, stats_in[...], squares)
+    near_in[mine] = near[...]
+    copies = []
+    for j, peer in enumerate(group):
+        copies.append(remote(near, near_in.at[mine], ns.at[j], nr.at[mine], peer))
+        copies[-1].start()
+    for j, peer in enumerate(group):
+        slot = peer["role"] * groups + peer["mp"]
+        remote(near, near_in.at[slot], ns.at[j], nr.at[slot], peer).wait_recv()
+    for copy in copies:
+        copy.wait_send()
+    summed = near_in[0]
+    for j in range(1, 2 * groups):
+        summed += near_in[j]
+    near[...] = summed
+    far_in[d] = summed
+    copies = []
+    for j, peer in enumerate(far):
+        copies.append(remote(near, far_in.at[d], fs.at[j], fr.at[d], peer))
+        copies[-1].start()
+    for j, peer in enumerate(far):
+        slot = peer["dp"]
+        remote(near, far_in.at[slot], fs.at[j], fr.at[slot], peer).wait_recv()
+    for copy in copies:
+        copy.wait_send()
+    summed = far_in[0]
+    for j in range(1, nz):
+        summed += far_in[j]
+    stats_out[...] = summed
+
+    for k in range(count):
+        for j in range(groups):
+            core(k, j).wait_send()
+
+        def done(piece, carry):
+            for copy in first(k, piece):
+                copy.wait_send()
+            for copy in second(k, piece):
+                copy.wait_send()
+
+            @pl.when(piece != d)
+            def _():
+                right(k, piece).wait_send()
+
+            return carry
+
+        lax.fori_loop(0, nz, done, 0)
+
+
+def reduce_all(grads, wire_types, stats):
+    nz = lax.axis_size("dp")
+    groups = lax.axis_size("mp")
+    count = len(grads)
+    dma = pltpu.SemaphoreType.DMA
+    shapes = [g.shape[2:] for g in grads]
+    vmem = pl.BlockSpec(memory_space=pltpu.VMEM)
+    scratch = (
+        [pltpu.VMEM((groups, nz, *s), jnp.float32) for s in shapes]
+        + [pltpu.VMEM((2, nz, *s), jnp.float32) for s in shapes]
+        + [pltpu.VMEM((nz, *s), t) for s, t in zip(shapes, wire_types)] * 2
+        + [pltpu.VMEM((2, nz, *s), t) for s, t in zip(shapes, wire_types)] * 2
+        + [pltpu.VMEM((nz + 1, *s), jnp.float32) for s in shapes]
+        + [
+            pltpu.VMEM((8, 128), jnp.float32),
+            pltpu.VMEM((2 * groups, 8, 128), jnp.float32),
+            pltpu.VMEM((nz, 8, 128), jnp.float32),
+            dma((count, 2)),
+            dma((count, groups)),
+            dma((count, groups)),
+            dma((count, 2, nz)),
+            dma((count, 2, nz)),
+            dma((count, 2, nz)),
+            dma((count, 2, nz)),
+            dma((count, nz)),
+            dma((count, nz + 1)),
+            dma((2 * groups,)),
+            dma((2 * groups,)),
+            dma((nz,)),
+            dma((nz,)),
+        ]
+    )
+    return pl.pallas_call(
+        functools.partial(reduce_kernel, nz, count),
+        out_shape=[jax.ShapeDtypeStruct(s, jnp.float32) for s in shapes]
+        + [jax.ShapeDtypeStruct((8, 128), jnp.float32)],
+        in_specs=[vmem] + [pl.BlockSpec(memory_space=pl.ANY)] * count,
+        out_specs=[vmem] * (count + 1),
+        scratch_shapes=scratch,
+        compiler_params=pltpu.CompilerParams(
+            collective_id=2, has_side_effects=True, vmem_limit_bytes=60 * 2**20
+        ),
+    )(stats, *grads)
+
+
 def encoder_forward(pix, place, keep, bank, gains, sizes, asked):
     local, hidden, pixel = sizes
     heads = HEADS // bank.shape[0]
@@ -181,7 +697,7 @@
     up = 4 * local
     down = up + hidden
     emb = down + hidden
-    start = dots("gnk,gdk->nd", pix, bank[:, :, emb:]) + place
+    start = dots("gnk,gdk->nd", pix, bank[:, :, emb : emb + pixel]) + place
     norm1, scale1 = layer_stats(start)
     mixer_in = (norm1 * gains[0]).astype(BF)
     triple = dots("nd,gdk->gnk", mixer_in, bank[:, :, : 3 * local]).astype(BF)
@@ -378,26 +894,30 @@
     patches = pixels.shape[1]
     image = lax.axis_index("role") * groups + lax.axis_index("mp")
 
-    def gather(packed):
-        whole = lax.all_gather(packed.astype(BF), EVERY, axis=0, tiled=True)
-        return whole.reshape(groups, -1, packed.shape[1])
-
-    bank = gather(pack_encoder(encoder_in, encoder_out, local, pixel))
-    pbank = gather(pack_predictor(predictor_in, predictor_out, local, plocal, phidden))
-    tbank = gather(pack_encoder(target_encoder_in, target_encoder_out, local, pixel))
-    both = lax.all_gather(
-        jnp.stack([vectors, target_vectors]).astype(BF), ("role", "dp", "mp"), axis=0
-    )
-    s_vec = both[:, 0].reshape(-1).astype(F32)
-    t_vec = both[:, 1].reshape(-1).astype(F32)
-    target_total = lax.psum(jnp.sum(target_count).astype(F32), "dp")
-
-    half = lax.dynamic_slice_in_dim(pixels, lax.axis_index("role") * groups, groups, 0)
-    pix = lax.all_to_all(half, "mp", 0, 0, tiled=True)
     slots = lax.dynamic_index_in_dim(context_slots, image, 0, keepdims=False)
     count = lax.dynamic_index_in_dim(context_count, image, 0, keepdims=False)
     tslots = lax.dynamic_index_in_dim(target_slots, image, 0, keepdims=False)
     tcount = lax.dynamic_index_in_dim(target_count, image, 0, keepdims=False)
+    tsum = jnp.broadcast_to(jnp.sum(tcount).astype(F32), vectors.shape)
+    gathered = gather_all(
+        [
+            pack_encoder(encoder_in, encoder_out, local, pixel, [vectors, tsum]),
+            pack_predictor(predictor_in, predictor_out, local, plocal, phidden),
+            pack_encoder(target_encoder_in, target_encoder_out, local, pixel, [target_vectors]),
+        ]
+    )
+    bank, pbank, tbank = (g.reshape(groups, -1, g.shape[-1]) for g in gathered)
+    extra = 4 * local + 2 * hidden + pixel
+
+    def spread_vector(whole):
+        return whole[:, :, extra].reshape(groups, owners, -1).transpose(1, 0, 2).reshape(-1)
+
+    s_vec = spread_vector(bank).astype(F32)
+    t_vec = spread_vector(tbank).astype(F32)
+    target_total = jnp.sum(gathered[0][:, :, 0, extra + 1].astype(F32))
+
+    half = lax.dynamic_slice_in_dim(pixels, lax.axis_index("role") * groups, groups, 0)
+    pix = lax.all_to_all(half, "mp", 0, 0, tiled=True)
     nctx = slots.shape[0]
     blocks, tlen = tslots.shape
 
@@ -441,15 +961,21 @@
     )
     g_vec = jnp.concatenate([g_first, g_second, *p_small])
 
-    def scatter(grads):
-        flat = grads.reshape(-1, grads.shape[-1])
-        return lax.psum_scatter(flat, EVERY, scatter_dimension=0, tiled=True)
-
-    r_pin, r_pout = unpack_predictor(scatter(g_pbank), local, plocal, phidden)
-    r_in, r_out = unpack_encoder(scatter(g_bank), local, hidden, pixel)
-    r_vec = lax.psum_scatter(g_vec, ("role", "dp", "mp"), scatter_dimension=0, tiled=True)
-    squares = sum(jnp.sum(g * g) for g in (r_in, r_out, r_pin, r_pout, r_vec))
-    squares, loss_total = lax.psum((squares, loss), ("role", "dp", "mp"))
+    small = g_vec.reshape(owners, groups, -1).transpose(1, 0, 2).reshape(groups, width, 1)
+    rest = jnp.zeros((groups, width, bank.shape[2] - extra - 1), F32)
+    g_bank = jnp.concatenate([g_bank, small, rest], 2)
+    r_bank, r_pbank, stats = reduce_all(
+        [
+            g_bank.reshape(gathered[0].shape),
+            g_pbank.reshape(gathered[1].shape),
+        ],
+        (BF, F32),
+        jnp.broadcast_to(loss, (8, LANES)),
+    )
+    r_pin, r_pout = unpack_predictor(r_pbank, local, plocal, phidden)
+    r_in, r_out = unpack_encoder(r_bank, local, hidden, pixel)
+    r_vec = r_bank[:, extra]
+    loss_total, squares = (stats[0, 0], stats[1, 0])
     grad_norm = jnp.sqrt(squares)
     scale = jnp.minimum(1.0, CLIP / (grad_norm + 1e-06))
     new_in, m_in, v_in = adamw(

time: 935 us -> 639 us (0.68)
  waiting for transfers between devices: 459 us -> 0.01 us
  Pallas kernels: 0 us -> 310 us
  blocking collectives: 158 us -> 0 us
  local copies, waits for them, and re-layouts: 90.3 us -> 122 us
  between operations: 22.2 us -> 5.79 us
    pallas_call x0 -> x2, Pallas kernels: none -> 310 us  [the longest x1 162 us: gather_all(): pl.pallas_call(functools.partial(gather_kernel, nz, count), out_shape=[ja...]
    reduce_scatter x2 -> x0, waiting for transfers between devices: 294 us -> none  [scatter(): return lax.psum_scatter(flat, EVERY, scatter_dimension=0, tiled=True)]
    all_gather x3 -> x0, waiting for transfers between devices: 165 us -> none  [gather(): whole = lax.all_gather(packed.astype(BF), EVERY, axis=0, tiled=True)]
    all_gather x1 -> x0, blocking collectives: 65.6 us -> none  [per_device(): lax.all_gather(jnp.stack([vectors, target_vectors]).astype(BF), ('role',...]
    psum x2 -> x0, blocking collectives: 53 us -> none  [the longest x1 40.4 us: per_device(): squares, loss_total = lax.psum((squares, loss), ('role', 'dp', 'mp'))]
    unnamed x1 -> x0, blocking collectives: 39 us -> none
    transpose x0 -> x3, local copies, waits for them, and re-layouts: none -> 14.5 us  [dots(): return jnp.einsum(spec, left, right, preferred_element_type=F32)]
    concatenate x2 -> x3, local copies, waits for them, and re-layouts: 30.8 us -> 36.4 us  [the longest x2 36.3 us: per_device(): g_bank = jnp.concatenate([g_bank, small, rest], 2)]
  transfers between devices with their start and end apart: 6 -> 1, of which waited for: 5 -> 0; matrix products, arithmetic and copies ran while one was open for 14% -> 3% of each run, Pallas kernels for 0% -> 26%
where the time goes in v2:
time: 639 us; the launch traced here: 633 us
  Pallas kernels  310 us (49%)
  matrix products  142 us (22%)
  local copies, waits for them, and re-layouts  122 us (19%)
  other arithmetic  47.7 us (7%)
    pallas_call x1, Pallas kernels, gather_all(): pl.pallas_call(functools.partial(gather_kernel, nz, count), out_shape=[ja...  162 us
    pallas_call x1, Pallas kernels, reduce_all(): pl.pallas_call(functools.partial(reduce_kernel, nz, count), out_shape=[ja...  149 us
    dot_general x58, matrix products, dots(): return jnp.einsum(spec, left, right, preferred_element_type=F32)  134 us
    concatenate x2, local copies, waits for them, and re-layouts, per_device(): g_bank = jnp.concatenate([g_bank, small, rest], 2)  36.3 us
    sub x1, other arithmetic, predictor(): grad_probs - jnp.sum(grad_probs * probs32, -1, keepdims=True)  20.7 us
    transpose x3, local copies, waits for them, and re-layouts, dots(): return jnp.einsum(spec, left, right, preferred_element_type=F32)  14.5 us
  transfers between devices with their start and end apart: 1, of which 0 were waited for; matrix products, arithmetic and copies ran while one was open for 3% of the time, Pallas kernels for 26%

profile of v2, /device:TPU:0, one launch (start us, length us, event | category | flops | bytes accessed | tf_op | source)
XLA Modules:
  0.0 633.1 jit_solution(2061659873201449121)
XLA Ops:
  2.6 5.3 all-to-all-start
  20.1 161.7 %shard_map.400 = (bf16[4,8,96,2560]{3,2,1,0:T(8,128)(2,1)}, bf16[4,8,48,1536]{3,2,1,0:T(8,128)(2,1)}, bf16[4,8,96,2560]{3,2,1,0:T(8,128)(2,1)}) custom-call(bf16[96,2560]{1,0:T(8,128)(2,1)} %concatenate.77.refs_0_, bf16[48,1536]{1,0:T(8,128)(2,1)} %concatenate.78.refs_1_, bf16[96,2560]{1,0:T(8,128)(2,1)} %concatenate.79.refs_2_), custom_call_target="tpu_custom_call" | custom-call | tf_op jit(solution)/shard_map/pallas_call | solution.py:386
  195.5 3.1 fusion.85
  204.4 3.0 fusion.369
  207.7 3.3 fusion.13
  212.3 4.0 fusion.160
  219.4 2.6 fusion.71
  222.3 2.5 fusion.359
  225.0 3.1 fusion.82
  234.4 3.5 fusion.360
  240.1 2.9 fusion.361
  244.0 6.8 %fusion.362 = (f32[196]{0:T(256)S(1)}, f32[196,768]{1,0:T(8,128)S(1)}) fusion(f32[196,768]{1,0:T(8,128)} %copy-done.35, bf16[4,768,2560]{2,1,0:T(8,128)(2,1)} %bitcast.441, f32[768]{0:T(1024)S(1)} %copy-done.125, f32[196]{0:T(256)S(1)} %add_rsqrt_fusion.2, f32[196]{0:T(256)S(1)} %broadcast_multiply_fusion.15), kind=kOutput, calls=%fused_computation.468 | convolution fusion | flops 1853601536 | bytes 11273520 | tf_op jit(solution)/shard_map/gnk,gdk->nd/dot_general | solution.py:32
  269.9 2.6 fusion.373
  282.9 2.7 convert_reduce_fusion.2
  288.5 20.7 %multiply_convert_fusion = bf16[4,3,4,64,224]{4,3,2,1,0:T(8,128)(2,1)S(1)} fusion(f32[4,3,4,64,64]{4,3,2,1,0:T(8,128)S(1)} %fusion.222, f32[4,3,4,64,160]{4,3,2,1,0:T(8,128)S(1)} %fusion.224, f32[4,3,4,64]{3,2,1,0:T(4,128)S(1)} %fusion.70, f32[4,3,4,64]{3,2,1,0:T(4,128)S(1)} %reduce_max.41, f32[4,3,4,64,64]{4,3,2,1,0:T(8,128)S(1)} %get-tuple-element.116, ...), kind=kOutput, calls=%fused_computation.24 | output fusion | flops 8260831 | bytes 6905856 | tf_op jit(solution)/shard_map/sub | solution.py:816
  316.4 2.4 convolution_bitcast_fusion.18
  335.7 4.4 fusion.34
  340.1 4.5 multiply_reduce_fusion.14
  344.9 3.2 fusion.163
  350.0 2.8 convolution_convert_fusion.1
  352.8 3.2 multiply_reduce_fusion.2
  365.1 4.7 multiply_reduce_fusion.6
  369.7 4.5 convolution_bitcast_fusion
  374.3 5.0 fusion.262
  379.3 5.1 fusion.326
  386.7 3.2 convolution_bitcast_fusion.1
  389.8 3.6 copy.250
  396.2 8.6 %copy.247 = f32[4,768,576]{2,1,0:T(8,128)} copy(f32[4,768,576]{1,2,0:T(8,128)} %convolution_bitcast_fusion) | data formatting | bytes 14155776 | tf_op jit(solution)/shard_map/nd,gnk->gdk/transpose | solution.py:32
  404.9 3.0 fusion.72
  417.9 9.6 %copy.255 = f32[4,384,1536]{2,1,0:T(8,128)} copy(f32[4,384,1536]{1,2,0:T(8,128)} %fusion.76) | data formatting | bytes 18874368 | tf_op jit(solution)/shard_map/concatenate | solution.py:857
  428.9 35.8 %concatenate.94.refs_0_ = f32[4,8,96,2560]{3,2,1,0:T(8,128)} concatenate(f32[4,8,96,576]{3,2,1,0:T(8,128)} %bitcast.399, f32[4,8,96,192]{3,2,1,0:T(8,128)} %bitcast.401, f32[4,8,96,768]{3,2,1,0:T(8,128)} %bitcast.396, f32[4,8,96,768]{3,2,1,0:T(8,128)} %bitcast.397, f32[4,8,96,192]{3,2,1,0:T(8,128)} %bitcast.400, f32[4,8,96,1]{3,2,1,0:T(8,128)S(1)} %copy.252, ...), dimensions={3} | concatenate | bytes 62914560 | tf_op jit(solution)/shard_map/concatenate | solution.py:966
  465.9 148.5 %shard_map.401 = (f32[96,2560]{1,0:T(8,128)}, f32[48,1536]{1,0:T(8,128)}, f32[8,128]{1,0:T(8,128)}) custom-call(f32[8,128]{1,0:T(8,128)} %broadcast_in_dim.49.stats_in, f32[4,8,96,2560]{3,2,1,0:T(8,128)} %concatenate.94.refs_0_, f32[4,8,48,1536]{3,2,1,0:T(8,128)} %bitcast.398), custom_call_target="tpu_custom_call" | custom-call | tf_op jit(solution)/shard_map/pallas_call | solution.py:680
  (512 shorter events, 147.4 us)
Async XLA Ops:
  0.7 14.5 %copy-start.74 = (f32[48,864]{1,0:T(8,128)S(1)}, f32[48,864]{1,0:T(8,128)}, u32[]{:S(2)}) copy-start(f32[48,864]{1,0:T(8,128)} %param.32) | copy-start | bytes 497668
  0.7 14.7 %copy-start.44 = (f32[1152,96]{0,1:T(8,128)S(1)}, f32[1152,96]{0,1:T(8,128)}, u32[]{:S(2)}) copy-start(f32[1152,96]{0,1:T(8,128)} %param.31) | copy-start | bytes 1327108
  0.7 14.8 %copy-start.46 = (f32[1152,96]{0,1:T(8,128)S(1)}, f32[1152,96]{0,1:T(8,128)}, u32[]{:S(2)}) copy-start(f32[1152,96]{0,1:T(8,128)} %param.46) | copy-start | bytes 1327108
  2.6 13.1 %copy-start.39 = (f32[96,1344]{1,0:T(8,128)S(1)}, f32[96,1344]{1,0:T(8,128)}, u32[]{:S(2)}) copy-start(f32[96,1344]{1,0:T(8,128)} %param.30) | copy-start | bytes 1548292
  2.6 189.5 %all-to-all-start = ((bf16[4,196,192]{1,2,0:T(8,128)(2,1)}), bf16[4,196,192]{1,2,0:T(8,128)(2,1)S(1)}, u32[]{:S(2)}, u32[]{:S(2)}) async-start(bf16[4,196,192]{1,2,0:T(8,128)(2,1)} %constant_dynamic-slice_fusion.1), calls=%async_computation | async-start | bytes 786432 | tf_op jit(solution)/shard_map/all_to_all | solution.py:920
  9.8 192.5 %copy-start.138 = (f32[196]{0:T(256)}, f32[196]{0:T(256)S(1)}, u32[]{:S(2)}) copy-start(f32[196]{0:T(256)S(1)} %fusion.303) | copy-start | bytes 2356
  19.1 172.5 %copy-start.66 = (f32[196,384]{1,0:T(8,128)S(1)}, f32[196,384]{1,0:T(8,128)}, u32[]{:S(2)}) copy-start(f32[196,384]{1,0:T(8,128)} %constant.96.clone) | copy-start | bytes 903172
  191.3 84.4 %copy-start.100 = (f32[384]{0:T(512)}, f32[384]{0:T(512)S(1)}, u32[]{:S(2)}) copy-start(f32[384]{0:T(512)S(1)} %slice.360) | copy-start | bytes 4612
  191.3 86.7 %copy-start.92 = (f32[384]{0:T(512)}, f32[384]{0:T(512)S(1)}, u32[]{:S(2)}) copy-start(f32[384]{0:T(512)S(1)} %slice.357) | copy-start | bytes 4612
  191.4 27.7 %copy-start.94 = (f32[384]{0:T(512)}, f32[384]{0:T(512)S(1)}, u32[]{:S(2)}) copy-start(f32[384]{0:T(512)S(1)} %slice.344) | copy-start | bytes 4612
  222.2 32.3 %copy-start.30 = (bf16[4,416,96]{1,2,0:T(8,128)(2,1)}, bf16[4,416,96]{1,2,0:T(8,128)(2,1)S(1)}, u32[]{:S(2)}) copy-start(bf16[4,416,96]{1,2,0:T(8,128)(2,1)S(1)} %get-tuple-element.73) | copy-start | bytes 958468
  222.2 33.7 %copy-start.29 = (bf16[4,416,96]{1,2,0:T(8,128)(2,1)}, bf16[4,416,96]{1,2,0:T(8,128)(2,1)S(1)}, u32[]{:S(2)}) copy-start(bf16[4,416,96]{1,2,0:T(8,128)(2,1)S(1)} %get-tuple-element.72) | copy-start | bytes 958468
  244.0 7.7 %copy-start.114 = (s32[256]{0:T(256)S(1)}, s32[256]{0:T(256)}, u32[]{:S(2)}) copy-start(s32[256]{0:T(256)} %copy-done.113) | copy-start | bytes 3076
  254.8 8.4 %copy-start.20 = (bf16[4,4,64,3,32]{2,1,4,3,0:T(4,128)(2,1)}, bf16[4,4,64,3,32]{2,1,4,3,0:T(4,128)(2,1)S(1)}, u32[]{:S(2)}) copy-start(bf16[4,4,64,3,32]{2,1,4,3,0:T(4,128)(2,1)S(1)} %reshape.426) | copy-start | bytes 589828
  267.6 10.4 %copy-start.98 = (f32[256]{0:T(256)}, f32[256]{0:T(256)S(1)}, u32[]{:S(2)}) copy-start(f32[256]{0:T(256)S(1)} %broadcast_multiply_fusion.8) | copy-start | bytes 3076
  267.8 10.2 %copy-start.108 = (f32[256]{0:T(256)}, f32[256]{0:T(256)S(1)}, u32[]{:S(2)}) copy-start(f32[256]{0:T(256)S(1)} %add_rsqrt_fusion.5) | copy-start | bytes 3076
  288.5 20.7 %copy-start.27 = (bf16[4,4,64,3,32]{2,1,4,3,0:T(4,128)(2,1)S(1)}, bf16[4,4,64,3,32]{2,1,4,3,0:T(4,128)(2,1)}, u32[]{:S(2)}) copy-start(bf16[4,4,64,3,32]{2,1,4,3,0:T(4,128)(2,1)} %reshape.425) | copy-start | bytes 589828
  323.1 7.0 %copy-start.84 = (bf16[4,256,96]{1,2,0:T(8,128)(2,1)}, bf16[4,256,96]{1,2,0:T(8,128)(2,1)S(1)}, u32[]{:S(2)}) copy-start(bf16[4,256,96]{1,2,0:T(8,128)(2,1)S(1)} %reshape.438) | copy-start | bytes 589828
  379.3 7.2 %copy-start.112 = (f32[3072]{0:T(1024)S(1)}, f32[3072]{0:T(1024)}, u32[]{:S(2)}) copy-start(f32[3072]{0:T(1024)} %custom-call.1) | copy-start | bytes 36868
  379.3 7.2 %copy-start.128 = (f32[384]{0:T(512)S(1)}, f32[384]{0:T(512)}, u32[]{:S(2)}) copy-start(f32[384]{0:T(512)} %get-tuple-element.41) | copy-start | bytes 4612
  379.3 7.2 %copy-start.127 = (f32[384]{0:T(512)S(1)}, f32[384]{0:T(512)}, u32[]{:S(2)}) copy-start(f32[384]{0:T(512)} %get-tuple-element.39) | copy-start | bytes 4612
  396.2 8.6 %slice-start.2 = ((bf16[416,384]{1,0:T(8,128)(2,1)}), bf16[160,384]{1,0:T(8,128)(2,1)S(1)}, s32[]{:S(2)}) async-start(bf16[416,384]{1,0:T(8,128)(2,1)} %copy-done.64), calls=%async_computation.3 | async-start | bytes 245760 | tf_op jit(solution)/shard_map/slice | solution.py:837
  396.2 8.6 %copy-start.81 = (bf16[4,160,192]{1,2,0:T(8,128)(2,1)S(1)}, bf16[4,160,192]{1,2,0:T(8,128)(2,1)}, u32[]{:S(2)}) copy-start(bf16[4,160,192]{1,2,0:T(8,128)(2,1)} %copy.254) | copy-start | bytes 737284
  396.2 8.6 %copy-start.85 = (bf16[4,256,96]{1,2,0:T(8,128)(2,1)S(1)}, bf16[4,256,96]{1,2,0:T(8,128)(2,1)}, u32[]{:S(2)}) copy-start(bf16[4,256,96]{1,2,0:T(8,128)(2,1)} %copy-done.84) | copy-start | bytes 589828
  614.4 10.6 %copy-start.133 = (f32[96]{0:T(128)S(1)}, f32[96]{0:T(128)}, u32[]{:S(2)}) copy-start(f32[96]{0:T(128)} %param.34) | copy-start | bytes 1156
  614.4 10.6 %copy-start.135 = (f32[96]{0:T(128)S(1)}, f32[96]{0:T(128)}, u32[]{:S(2)}) copy-start(f32[96]{0:T(128)} %param.47) | copy-start | bytes 1156
  614.4 10.6 %copy-start.136 = (f32[96]{0:T(128)S(1)}, f32[96]{0:T(128)}, u32[]{:S(2)}) copy-start(f32[96]{0:T(128)} %param.39) | copy-start | bytes 1156
  614.4 10.6 %copy-start.137 = (f32[96]{0:T(128)S(1)}, f32[96]{0:T(128)}, u32[]{:S(2)}) copy-start(f32[96]{0:T(128)} %param.44) | copy-start | bytes 1156
  614.5 11.2 %copy-start.45 = (f32[1152,96]{0,1:T(8,128)S(1)}, f32[1152,96]{0,1:T(8,128)}, u32[]{:S(2)}) copy-start(f32[1152,96]{0,1:T(8,128)} %param.31) | copy-start | bytes 1327108
  614.5 11.2 %copy-start.47 = (f32[1152,96]{0,1:T(8,128)S(1)}, f32[1152,96]{0,1:T(8,128)}, u32[]{:S(2)}) copy-start(f32[1152,96]{0,1:T(8,128)} %param.46) | copy-start | bytes 1327108
  614.5 11.2 %copy-start.79 = (f32[1152,96]{0,1:T(8,128)S(1)}, f32[1152,96]{0,1:T(8,128)}, u32[]{:S(2)}) copy-start(f32[1152,96]{0,1:T(8,128)} %param.36) | copy-start | bytes 1327108
  614.5 11.2 %copy-start.80 = (f32[1152,96]{0,1:T(8,128)S(1)}, f32[1152,96]{0,1:T(8,128)}, u32[]{:S(2)}) copy-start(f32[1152,96]{0,1:T(8,128)} %param.41) | copy-start | bytes 1327108
  (112 other events, 339.9 us)

commit v3 on v2

--- a/solution.py
+++ b/solution.py
@@ -28,10 +28,6 @@
 LANES = 128
 
 
-def dots(spec, left, right):
-    return jnp.einsum(spec, left, right, preferred_element_type=F32)
-
-
 def sincos(width):
     quarter = width // 4
     omega = 1.0 / 10000.0 ** (np.arange(quarter, dtype=np.float64) / quarter)
@@ -44,37 +40,14 @@
 
 
 def pick(table, places):
-    hot = (places[:, None] == jnp.arange(table.shape[0])[None, :]).astype(F32)
-    return jnp.dot(hot, table, precision=lax.Precision.HIGHEST, preferred_element_type=F32)
-
-
-def layer_stats(stream):
-    mean = jnp.mean(stream, -1, keepdims=True)
-    cent = stream - mean
-    scale = lax.rsqrt(jnp.mean(cent * cent, -1, keepdims=True) + 1e-06)
-    return (cent * scale, scale)
-
-
-def norm_back(normed, scale, gain, grad):
-    gain_grad = jnp.sum(grad * normed, 0)
-    scaled = grad * gain
-    inner = (
-        scaled
-        - jnp.mean(scaled, -1, keepdims=True)
-        - normed * jnp.mean(scaled * normed, -1, keepdims=True)
-    )
-    return (scale * inner, gain_grad)
-
-
-def gelu(hidden):
-    return 0.5 * hidden * (1.0 + lax.erf(hidden * ROOT_HALF))
-
-
-def gelu_slope(hidden):
-    return (
-        0.5 * (1.0 + lax.erf(hidden * ROOT_HALF))
-        + hidden * jnp.exp(-0.5 * hidden * hidden) * INVERSE_ROOT
-    )
+    parts, rest = ([], table)
+    for _ in range(3):
+        parts.append(rest.astype(jnp.bfloat16))
+        rest = rest - parts[-1].astype(np.float32)
+    hot = (places[:, None] == jnp.arange(table.shape[0])[None, :]).astype(BF)
+    rows = jnp.dot(hot, np.concatenate(parts, 1), preferred_element_type=F32)
+    width = table.shape[1]
+    return rows[:, :width] + rows[:, width : 2 * width] + rows[:, 2 * width :]
 
 
 def pack_encoder(w_in, w_out, local, pixel, extras):
@@ -145,40 +118,6 @@
         first,
         second,
     )
-
-
-def split_heads(packed, heads):
-    groups, rows, cols = packed.shape
-    return packed.reshape(groups, rows, heads, cols // heads)
-
-
-def merge_heads(split):
-    groups, rows, heads, size = split.shape
-    return split.reshape(groups, rows, heads * size)
-
-
-def rest_forward(stream, mixed, w_o, w_up, w_down, second):
-    middle = stream + dots("gnk,gdk->nd", mixed, w_o)
-    norm2, scale2 = layer_stats(middle)
-    dense = (norm2 * second).astype(BF)
-    hidden = dots("nd,gdk->gnk", dense, w_up)
-    active = gelu(hidden).astype(BF)
-    out = middle + dots("gnk,gdk->nd", active, w_down)
-    return (out, (norm2, scale2, dense, hidden, active))
-
-
-def rest_backward(grad_out, saved, mixed, w_o, w_up, w_down, second):
-    norm2, scale2, dense, hidden, active = saved
-    branch = grad_out.astype(BF)
-    g_down = dots("nd,gnk->gdk", branch, active)
-    grad_hidden = (dots("nd,gdk->gnk", branch, w_down) * gelu_slope(hidden)).astype(BF)
-    g_up = dots("nd,gnk->gdk", dense, grad_hidden)
-    grad_norm, g_second = norm_back(norm2, scale2, second, dots("gnk,gdk->nd", grad_hidden, w_up))
-    grad_mid = grad_out + grad_norm
-    mixer = grad_mid.astype(BF)
-    g_o = dots("nd,gnk->gdk", mixer, mixed)
-    grad_mixed = dots("nd,gdk->gnk", mixer, w_o).astype(BF)
-    return (grad_mid, grad_mixed, g_o, g_up, g_down, g_second)
 
 
 def shift_of(rank, by):
@@ -690,172 +629,497 @@
     )(stats, *grads)
 
 
-def encoder_forward(pix, place, keep, bank, gains, sizes, asked):
-    local, hidden, pixel = sizes
-    heads = HEADS // bank.shape[0]
-    size = local // heads
+def dot(left, right):
+    return lax.dot_general(left, right, (((1,), (0,)), ((), ())), preferred_element_type=F32)
+
+
+def dot_rt(left, right):
+    return lax.dot_general(left, right, (((1,), (1,)), ((), ())), preferred_element_type=F32)
+
+
+def dot_lt(left, right):
+    return lax.dot_general(left, right, (((0,), (0,)), ((), ())), preferred_element_type=F32)
+
+
+def chain(term, count):
+    total = term(0)
+    for g in range(1, count):
+        total += term(g)
+    return total
+
+
+def head_lanes(lanes, size, head):
+    lane = lax.broadcasted_iota(jnp.int32, (1, lanes), 1)
+    return jnp.logical_and(lane >= head * size, lane < (head + 1) * size)
+
+
+def only(mask, value):
+    return jnp.where(mask, value, jnp.zeros_like(value))
+
+
+def turn(value, by):
+    return pltpu.roll(value, by % value.shape[1], 1)
+
+
+def stats_of(stream):
+    mean = jnp.mean(stream, -1, keepdims=True)
+    cent = stream - mean
+    scale = lax.rsqrt(jnp.mean(cent * cent, -1, keepdims=True) + 1e-06)
+    return (cent * scale, scale)
+
+
+def norm_back_of(normed, scale, gain, grad):
+    gain_grad = jnp.sum(grad * normed, 0, keepdims=True)
+    scaled = grad * gain
+    inner = (
+        scaled
+        - jnp.mean(scaled, -1, keepdims=True)
+        - normed * jnp.mean(scaled * normed, -1, keepdims=True)
+    )
+    return (scale * inner, gain_grad)
+
+
+def normal_cdf(hidden):
+    return 0.5 * (1.0 + lax.erf(hidden * ROOT_HALF))
+
+
+def encoder_kernel(sizes, asked, saving, pix, place, bias, bank, gains, *refs):
+    local, hidden, size = sizes
+    groups = bank.shape[0]
+    heads = local // size
     up = 4 * local
     down = up + hidden
     emb = down + hidden
-    start = dots("gnk,gdk->nd", pix, bank[:, :, emb : emb + pixel]) + place
-    norm1, scale1 = layer_stats(start)
-    mixer_in = (norm1 * gains[0]).astype(BF)
-    triple = dots("nd,gdk->gnk", mixer_in, bank[:, :, : 3 * local]).astype(BF)
-    queries = split_heads(triple[:, :asked, :local], heads)
-    keyset = split_heads(triple[:, :, local : 2 * local], heads)
-    values = split_heads(triple[:, :, 2 * local :], heads)
-    score = dots("gnhs,gmhs->ghnm", queries, keyset) * size**-0.5 + (keep - 1.0) * 1e9
-    probs32 = jax.nn.softmax(score, -1)
-    probs = probs32.astype(BF)
-    mixed = merge_heads(dots("ghnm,gmhs->gnhs", probs, values).astype(BF))
-    out, rest = rest_forward(
-        start[:asked], mixed, bank[:, :, 3 * local : up], bank[:, :, up:down],
-        bank[:, :, down:emb], gains[1],
-    )
-    return (out, (norm1, scale1, mixer_in, queries, keyset, values, probs32, mixed, rest))
-
-
-def encoder_backward(grad_out, saved, pix, bank, gains, sizes):
-    norm1, scale1, mixer_in, queries, keyset, values, probs32, mixed, rest = saved
-    local, hidden, pixel = sizes
-    asked = queries.shape[1]
-    size = queries.shape[3]
-    up = 4 * local
-    down = up + hidden
-    emb = down + hidden
-    heads = queries.shape[2]
-    grad_mid, grad_mixed, g_o, g_up, g_down, g_second = rest_backward(
-        grad_out, rest, mixed, bank[:, :, 3 * local : up], bank[:, :, up:down],
-        bank[:, :, down:emb], gains[1],
-    )
-    grad_mixed = split_heads(grad_mixed, heads)
-    probs = probs32.astype(BF)
-    grad_probs = dots("gnhs,gmhs->ghnm", grad_mixed, values)
-    grad_values = dots("ghnm,gnhs->gmhs", probs, grad_mixed).astype(BF)
-    grad_scores = (
-        probs32 * (grad_probs - jnp.sum(grad_probs * probs32, -1, keepdims=True))
-    ).astype(BF)
-    grad_queries = (dots("ghnm,gmhs->gnhs", grad_scores, keyset) * size**-0.5).astype(BF)
-    grad_keys = (dots("ghnm,gnhs->gmhs", grad_scores, queries) * size**-0.5).astype(BF)
-    total = mixer_in.shape[0]
-    grad_queries = jnp.pad(merge_heads(grad_queries), ((0, 0), (0, total - asked), (0, 0)))
-    triple = jnp.concatenate([grad_queries, merge_heads(grad_keys), merge_heads(grad_values)], 2)
-    g_qkv = dots("nd,gnk->gdk", mixer_in, triple)
-    grad_norm, g_first = norm_back(
-        norm1, scale1, gains[0], dots("gnk,gdk->nd", triple, bank[:, :, : 3 * local])
-    )
-    grad_start = (jnp.pad(grad_mid, ((0, total - asked), (0, 0))) + grad_norm).astype(BF)
-    g_emb = dots("nd,gnk->gdk", grad_start, pix)
-    return (jnp.concatenate([g_qkv, g_o, g_up, g_down, g_emb], 2), g_first, g_second)
-
-
-def predictor(context, targets, table, slots, tslots, ckeep, tkeep, total, bank, gains, sizes):
-    local, plocal, phidden = sizes
-    first, second, final, token = gains
-    heads = HEADS // bank.shape[0]
-    size = plocal // heads
+    wide = local + 64
+    if saving:
+        (out, norm1, scale1, mixer_in, qs, ks, vs, probs_out, mixed_out, norm2, scale2, dense,
+         slope, active) = refs
+    else:
+        hot, out = refs[:2]
+    start = place[...] + chain(lambda g: dot_rt(pix[g], bank[g, :, emb : emb + wide]), groups)
+    normed, scale = stats_of(start)
+    a = (normed * gains[0:1]).astype(BF)
+    if saving:
+        norm1[...] = normed
+        scale1[...] = scale
+        mixer_in[...] = a
+    def attend(g):
+        t = dot(a, bank[g, :, : 3 * local + 64]).astype(BF).astype(F32)
+        q = t[:asked, :wide].astype(BF)
+        k = turn(t, -local)[:, :wide].astype(BF)
+        v = t[:, 2 * local :].astype(BF)
+        if saving:
+            qs[g] = q
+            ks[g] = k
+            vs[g] = v
+        mixed = jnp.zeros((asked, wide), F32)
+        for h in range(heads):
+            mask = head_lanes(wide, size, h)
+            score = dot_rt(only(mask, q), k) * size**-0.5 + bias[...]
+            score = jnp.exp(score - jnp.max(score, -1, keepdims=True))
+            probs = score / jnp.sum(score, -1, keepdims=True)
+            if saving:
+                probs_out[g * heads + h] = probs
+            mixed += only(mask, dot(probs.astype(BF), v))
+        mixed = turn(mixed, 64).astype(BF)
+        if saving:
+            mixed_out[g] = mixed
+        return dot_rt(mixed, bank[g, :, up - wide : up])
+
+    middle = start[:asked] + chain(attend, groups)
+    normed, scale = stats_of(middle)
+    b = (normed * gains[1:2]).astype(BF)
+    if saving:
+        norm2[...] = normed
+        scale2[...] = scale
+        dense[...] = b
+
+    def feed(g):
+        pre = dot(b, bank[g, :, up:down])
+        cdf = normal_cdf(pre)
+        act = (pre * cdf).astype(BF)
+        if saving:
+            slope[g] = cdf + pre * jnp.exp(-0.5 * pre * pre) * INVERSE_ROOT
+            active[g] = act
+        return dot_rt(act, bank[g, :, down:emb])
+
+    latent = middle + chain(feed, groups)
+    lane = lax.broadcasted_iota(jnp.int32, (1, wide), 1)
+    if saving:
+        for g in range(groups):
+            part = turn(latent, 64 - g * local)[:, :wide]
+            out[g] = only(lane >= 64, part).astype(BF)
+    else:
+        t_norm = stats_of(latent)[0].astype(BF)
+        chosen = dot(hot[...], t_norm)
+        for g in range(groups):
+            out[g] = turn(chosen, -g * local)[:, :wide].astype(BF)
+
+
+def run_encoder(pix, place, keep, bank, gains, sizes, asked, hot=None):
+    local, hidden, size = sizes
+    groups, width, _ = bank.shape
+    rows = place.shape[0]
+    wide = local + 64
+    heads = HEADS
+    bias = ((keep - 1.0) * 1e9)[None, :]
+    saving = hot is None
+    make = jax.ShapeDtypeStruct
+    if saving:
+        outs = [
+            make((groups, asked, wide), BF),
+            make((rows, width), F32),
+            make((rows, 1), F32),
+            make((rows, width), BF),
+            make((groups, asked, wide), BF),
+            make((groups, rows, wide), BF),
+            make((groups, rows, wide), BF),
+            make((heads, asked, rows), F32),
+            make((groups, asked, wide), BF),
+            make((asked, width), F32),
+            make((asked, 1), F32),
+            make((asked, width), BF),
+            make((groups, asked, hidden), F32),
+            make((groups, asked, hidden), BF),
+        ]
+    else:
+        outs = [make((groups, hot.shape[0], wide), BF)]
+    ins = [pix, place, bias, bank, gains] + ([] if saving else [hot])
+    vmem = pl.BlockSpec(memory_space=pltpu.VMEM)
+    return pl.pallas_call(
+        functools.partial(encoder_kernel, sizes, asked, saving),
+        out_shape=outs,
+        in_specs=[vmem] * len(ins),
+        out_specs=[vmem] * len(outs),
+        compiler_params=pltpu.CompilerParams(vmem_limit_bytes=56 * 2**20),
+    )(*ins)
+
+
+def predictor_kernel(
+    sizes, ctx, wanted, place_c, place_t, bias, weight, total, bank, gains,
+    grad_ctx, grads, small, loss_out, probs_s, q_s, k_s, v_s, mixed_s, slope_s, active_s, dt_s
+):
+    local, plocal, phidden, size, blocks = sizes
+    groups = bank.shape[0]
+    heads = plocal // size
+    lanes = 128
     up = 4 * plocal
     down = up + phidden
     head_at = down + phidden
     entry_at = head_at + local
-    w_qkv = bank[:, :, : 3 * plocal]
-    w_o = bank[:, :, 3 * plocal : up]
-    w_up = bank[:, :, up:down]
-    w_down = bank[:, :, down:head_at]
-    w_head = bank[:, :, head_at:entry_at]
-    w_entry = bank[:, :, entry_at:]
+    wide = local + 64
+    nctx = place_c.shape[0]
+    asked = place_t.shape[0]
+    rows = nctx + asked
+    tlen = asked // blocks
+    first, second, final, token = (gains[i : i + 1] for i in range(4))
+    root = size**-0.5
+
+    entry = place_c[...] + chain(
+        lambda g: dot_rt(ctx[g], bank[g, :, entry_at - 64 : entry_at + local]), groups
+    )
+    tgt_in = place_t[...] + token
+    norm_c, scale_c = stats_of(entry)
+    norm_t, scale_t = stats_of(tgt_in)
+    a_c = (norm_c * first).astype(BF)
+    a_t = (norm_t * first).astype(BF)
+    a = jnp.concatenate([a_c, a_t], 0)
+
+    def attend(g):
+        t = dot(a, bank[g, :, :up]).astype(BF).astype(F32)
+        q = t[nctx:, :lanes].astype(BF)
+        k = turn(t, -plocal)[:, :lanes].astype(BF)
+        v = turn(t, -2 * plocal)[:, :lanes].astype(BF)
+        q_s[g] = q
+        k_s[g] = k
+        v_s[g] = v
+        mixed = jnp.zeros((asked, lanes), F32)
+        for h in range(heads):
+            mask = head_lanes(lanes, size, h)
+            score = dot_rt(only(mask, q), k) * root + bias[...]
+            score = jnp.exp(score - jnp.max(score, -1, keepdims=True))
+            probs = score / jnp.sum(score, -1, keepdims=True)
+            probs_s[g * heads + h] = probs
+            mixed += only(mask, dot(probs.astype(BF), v))
+        mixed = turn(mixed, lanes - plocal).astype(BF)
+        mixed_s[g] = mixed
+        return dot_rt(mixed, bank[g, :, up - lanes : up])
+
+    middle = tgt_in + chain(attend, groups)
+    norm2, scale2 = stats_of(middle)
+    b = (norm2 * second).astype(BF)
+
+    def feed(g):
+        pre = dot(b, bank[g, :, up:down])
+        cdf = normal_cdf(pre)
+        slope_s[g] = cdf + pre * jnp.exp(-0.5 * pre * pre) * INVERSE_ROOT
+        act = (pre * cdf).astype(BF)
+        active_s[g] = act
+        return dot_rt(act, bank[g, :, down:head_at])
+
+    out = middle + chain(feed, groups)
+    norm_f, scale_f = stats_of(out)
+    head_in = (norm_f * final).astype(BF)
+    lane = lax.broadcasted_iota(jnp.int32, (1, wide), 1)
+    losses = jnp.zeros((1, 1), F32)
+    row_weight = weight[...]
+
+    def judge(g):
+        nonlocal losses
+        pred = dot(head_in, bank[g, :, head_at : head_at + wide])
+        diff = only(lane < local, pred - wanted[g].astype(F32))
+        losses += jnp.sum(row_weight * diff * diff, keepdims=True)
+        grad = (2.0 * row_weight * diff / total[...]).astype(BF)
+        g_head = dot_lt(head_in, grad)
+        grads[g, :, head_at : head_at + lanes] = g_head[:, :lanes]
+        grads[g, :, head_at + lanes : head_at + wide] = g_head[:, lanes:]
+        return dot_rt(grad, bank[g, :, head_at : head_at + wide])
+
+    grad_out, g_final = norm_back_of(norm_f, scale_f, final, chain(judge, groups))
+    loss_out[...] = jnp.broadcast_to(losses, loss_out.shape)
+
+    branch = grad_out.astype(BF)
+
+    def feed_back(g):
+        grads[g, :, down:head_at] = dot_lt(branch, active_s[g])
+        grad_pre = (dot(branch, bank[g, :, down:head_at]) * slope_s[g]).astype(BF)
+        grads[g, :, up:down] = dot_lt(b, grad_pre)
+        return dot_rt(grad_pre, bank[g, :, up:down])
+
+    grad_norm, g_second = norm_back_of(norm2, scale2, second, chain(feed_back, groups))
+    grad_mid = grad_out + grad_norm
+    mixer = grad_mid.astype(BF)
+
+    def attend_back(g):
+        g_o = dot_lt(mixer, mixed_s[g])
+        gm = turn(dot(mixer, bank[g, :, up - lanes : up]), plocal - lanes).astype(BF)
+        q, k, v = (q_s[g], k_s[g], v_s[g])
+        valid = head_lanes(lanes, plocal, 0)
+        gm = only(valid, gm)
+        qv = only(valid, q)
+        block = lax.broadcasted_iota(jnp.int32, (asked, 1), 0) // tlen
+        q_spread = jnp.concatenate([only(block == i, qv) for i in range(blocks)], 1)
+        gm_spread = jnp.concatenate([only(block == i, gm) for i in range(blocks)], 1)
+        dqs, dkt, dvt, dkc, dvc = ([], [], [], [], [])
+        for h in range(heads):
+            mask = head_lanes(lanes, size, h)
+            masks = jnp.concatenate([mask] * blocks, 1)
+            probs = probs_s[g * heads + h]
+            gmh = only(mask, gm)
+            grad_probs = dot_rt(gmh, v)
+            ds = (probs * (grad_probs - jnp.sum(grad_probs * probs, -1, keepdims=True))).astype(BF)
+            pb = probs.astype(BF)
+            qh = only(mask, qv)
+            dqs.append(dot(ds, only(mask, k)))
+            dkt.append(dot_lt(ds[:, nctx:], qh))
+            dvt.append(dot_lt(pb[:, nctx:], gmh))
+            dkc.append(dot_lt(ds[:, :nctx], only(masks, q_spread)))
+            dvc.append(dot_lt(pb[:, :nctx], only(masks, gm_spread)))
+        dq = (sum(dqs[1:], dqs[0]) * root).astype(BF).astype(F32)
+        dk = (sum(dkt[1:], dkt[0]) * root).astype(BF).astype(F32)
+        dv = sum(dvt[1:], dvt[0]).astype(BF).astype(F32)
+        kc = (sum(dkc[1:], dkc[0]) * root).astype(BF).astype(F32)
+        vc = sum(dvc[1:], dvc[0]).astype(BF).astype(F32)
+        kc = chain(lambda i: kc[:, i * lanes : (i + 1) * lanes], blocks)
+        vc = chain(lambda i: vc[:, i * lanes : (i + 1) * lanes], blocks)
+
+        def lay(query, keyed, valued):
+            count = keyed.shape[0]
+            blank = jnp.zeros((count, up - lanes), F32)
+            wideq = 0.0 if query is None else jnp.concatenate([query, blank], 1)
+            return (
+                wideq
+                + turn(jnp.concatenate([keyed, blank], 1), plocal)
+                + turn(jnp.concatenate([valued, blank], 1), 2 * plocal)
+            )
+
+        dt_t = lay(dq, dk, dv).astype(BF)
+        dt_c = lay(None, kc, vc)
+        high = dt_c.astype(BF)
+        low = (dt_c - high.astype(F32)).astype(BF)
+        dt = jnp.concatenate([high, dt_t], 0)
+        dt_s[g] = jnp.concatenate([dt, low], 0)
+        g_qkv = dot_lt(jnp.concatenate([a, a_c], 0), jnp.concatenate([dt, low], 0))
+        grads[g, :, : up - lanes] = g_qkv[:, : up - lanes]
+        grads[g, :, up - lanes : up] = g_qkv[:, up - lanes :] + g_o
+
+    for g in range(groups):
+        attend_back(g)
+    grad_a = chain(lambda g: dot_rt(dt_s[g], bank[g, :, :up]), groups)
+    grad_in_t, g_first_t = norm_back_of(norm_t, scale_t, first, grad_a[nctx:rows])
+    grad_in_c, g_first_c = norm_back_of(
+        norm_c, scale_c, first, grad_a[:nctx] + grad_a[rows:]
+    )
+    g_token = jnp.sum(grad_in_t + grad_mid, 0, keepdims=True)
+    small[...] = jnp.concatenate([g_first_t + g_first_c, g_second, g_final, g_token], 0)
+    grad_entry = grad_in_c.astype(BF)
+    width = groups * local
+    grad_context = jnp.zeros((nctx, width), F32)
+    for g in range(groups):
+        g_entry = dot_lt(grad_entry, ctx[g])
+        grads[g, :, entry_at - 64 : entry_at + 64] += g_entry[:, :lanes]
+        grads[g, :, entry_at + 64 : entry_at + local] = g_entry[:, lanes:]
+        part = only(lane >= 64, dot(grad_entry, bank[g, :, entry_at - 64 : entry_at + local]))
+        full = jnp.concatenate([part, jnp.zeros((nctx, width - wide), F32)], 1)
+        grad_context += turn(full, g * local - 64)
+    grad_ctx[...] = grad_context
+
+
+def run_predictor(ctx, wanted, place_c, place_t, bias, weight, total, bank, gains, sizes):
+    local, plocal, phidden, size, blocks = sizes
     groups = bank.shape[0]
-    blocks, tlen = tslots.shape
-    nctx = slots.shape[0]
-    asked = blocks * tlen
-    spread = context.reshape(nctx, groups, local).transpose(1, 0, 2)
-    entry = dots("gnk,gdk->nd", spread, w_entry) + pick(table, slots)
-    tgt_in = token + pick(table, tslots.reshape(-1))
-    norm1, scale1 = layer_stats(jnp.concatenate([entry, tgt_in], 0))
-    mixer_in = (norm1 * first).astype(BF)
-    triple = dots("nd,gdk->gnk", mixer_in, w_qkv).astype(BF)
-    queries = split_heads(triple[:, nctx:, :plocal], heads)
-    keyset = split_heads(triple[:, :, plocal : 2 * plocal], heads)
-    values = split_heads(triple[:, :, 2 * plocal :], heads)
-    shape_b = (groups, blocks, tlen, heads, size)
-    q_b = queries.reshape(shape_b)
-    k_c, v_c = (keyset[:, :nctx], values[:, :nctx])
-    k_t, v_t = (keyset[:, nctx:].reshape(shape_b), values[:, nctx:].reshape(shape_b))
-    s_c = dots("gbnhs,gmhs->ghbnm", q_b, k_c) * size**-0.5 + (ckeep - 1.0) * 1e9
-    s_t = (
-        dots("gbnhs,gbmhs->ghbnm", q_b, k_t) * size**-0.5 + (tkeep[:, None, :] - 1.0) * 1e9
-    )
-    score = jnp.concatenate([s_c, s_t], -1)
-    probs32 = jax.nn.softmax(score, -1)
-    probs = probs32.astype(BF)
-    mixed = dots("ghbnm,gmhs->gbnhs", probs[..., :nctx], v_c) + dots(
-        "ghbnm,gbmhs->gbnhs", probs[..., nctx:], v_t
-    )
-    mixed = mixed.astype(BF).reshape(groups, asked, plocal)
-    out, rest = rest_forward(tgt_in, mixed, w_o, w_up, w_down, second)
-    norm_f, scale_f = layer_stats(out)
-    head_in = (norm_f * final).astype(BF)
-    pred = dots("nd,gdk->gnk", head_in, w_head)
-    weight = tkeep.reshape(-1)[None, :, None]
-    wanted = targets.reshape(asked, groups, local).transpose(1, 0, 2).astype(F32)
-    diff = pred - wanted
-    loss = jnp.sum(weight * diff * diff)
-    grad_pred = (2.0 * weight * diff / total).astype(BF)
-    g_head = dots("nd,gnk->gdk", head_in, grad_pred)
-    grad_out, g_final = norm_back(
-        norm_f, scale_f, final, dots("gnk,gdk->nd", grad_pred, w_head)
-    )
-    grad_mid, grad_mixed, g_o, g_up, g_down, g_second = rest_backward(
-        grad_out, rest, mixed, w_o, w_up, w_down, second
-    )
-    gm = grad_mixed.reshape(shape_b)
-    grad_probs = jnp.concatenate(
-        [dots("gbnhs,gmhs->ghbnm", gm, v_c), dots("gbnhs,gbmhs->ghbnm", gm, v_t)], -1
-    )
-    grad_scores = (
-        probs32 * (grad_probs - jnp.sum(grad_probs * probs32, -1, keepdims=True))
+    nctx, pwidth = place_c.shape
+    asked = place_t.shape[0]
+    rows = nctx + asked
+    make = jax.ShapeDtypeStruct
+    outs = [
+        make((nctx, groups * local), F32),
+        make(bank.shape, F32),
+        make((4, pwidth), F32),
+        make((8, 128), F32),
+    ]
+    ins = [ctx, wanted, place_c, place_t, bias, weight, total, bank, gains]
+    vmem = pl.BlockSpec(memory_space=pltpu.VMEM)
+    scratch = [
+        pltpu.VMEM((HEADS, asked, rows), F32),
+        pltpu.VMEM((groups, asked, 128), BF),
+        pltpu.VMEM((groups, rows, 128), BF),
+        pltpu.VMEM((groups, rows, 128), BF),
+        pltpu.VMEM((groups, asked, 128), BF),
+        pltpu.VMEM((groups, asked, phidden), F32),
+        pltpu.VMEM((groups, asked, phidden), BF),
+        pltpu.VMEM((groups, rows + nctx, 4 * plocal), BF),
+    ]
+    return pl.pallas_call(
+        functools.partial(predictor_kernel, sizes),
+        out_shape=outs,
+        in_specs=[vmem] * len(ins),
+        out_specs=[vmem] * len(outs),
+        scratch_shapes=scratch,
+        compiler_params=pltpu.CompilerParams(vmem_limit_bytes=56 * 2**20),
+    )(*ins)
+
+
+def encoder_back_kernel(
+    sizes, grad_ctx, pix, norm1, scale1, mixer_in, qs, ks, vs, probs_in, mixed_in, norm2, scale2,
+    dense, slope, active, bank, gains, grads, small, wide_s, tail_s, dt_s, sems
+):
+    local, hidden, size = sizes
+    groups = bank.shape[0]
+    heads = local // size
+    up = 4 * local
+    down = up + hidden
+    emb = down + hidden
+    wide = local + 64
+    span = 3 * local + 64
+    asked = grad_ctx.shape[0]
+    rows = norm1.shape[0]
+    first, second = (gains[0:1], gains[1:2])
+    root = size**-0.5
+    grad_out = grad_ctx[...]
+    branch = grad_out.astype(BF)
+
+    def ship(g, start, width):
+        return pltpu.make_async_copy(
+            wide_s.at[g % 2, :, pl.ds(start, width)],
+            grads.at[g, :, pl.ds(start, width)],
+            sems.at[g % 2],
+        )
+
+    def feed_back(g):
+        if g >= 2:
+            ship(g - 2, up, 2 * hidden).wait()
+        wide_s[g % 2, :, down:emb] = dot_lt(branch, active[g])
+        grad_pre = (dot(branch, bank[g, :, down:emb]) * slope[g]).astype(BF)
+        wide_s[g % 2, :, up:down] = dot_lt(dense[...], grad_pre)
+        ship(g, up, 2 * hidden).start()
+        return dot_rt(grad_pre, bank[g, :, up:down])
+
+    grad_norm, g_second = norm_back_of(norm2[...], scale2[...], second, chain(feed_back, groups))
+    grad_mid = grad_out + grad_norm
+    mixer = grad_mid.astype(BF)
+    for g in range(groups - 2, groups):
+        ship(g, up, 2 * hidden).wait()
+    valid = head_lanes(wide, local, 0)
+
+    def attend_back(g):
+        g_o = dot_lt(mixer, mixed_in[g])
+        gm = turn(dot(mixer, bank[g, :, up - wide : up]), -64).astype(BF)
+        q, k, v = (only(valid, qs[g]), ks[g], vs[g])
+        gm = only(valid, gm)
+        dqs, dks, dvs = ([], [], [])
+        for h in range(heads):
+            mask = head_lanes(wide, size, h)
+            probs = probs_in[g * heads + h]
+            gmh = only(mask, gm)
+            grad_probs = dot_rt(gmh, v)
+            ds = (probs * (grad_probs - jnp.sum(grad_probs * probs, -1, keepdims=True))).astype(BF)
+            dqs.append(dot(ds, only(mask, k)))
+            dks.append(dot_lt(ds, only(mask, q)))
+            dvs.append(dot_lt(probs.astype(BF), gmh))
+        dq = (sum(dqs[1:], dqs[0]) * root).astype(BF).astype(F32)
+        dk = (sum(dks[1:], dks[0]) * root).astype(BF).astype(F32)
+        dv = sum(dvs[1:], dvs[0]).astype(BF).astype(F32)
+        dq = jnp.concatenate([dq, jnp.zeros((rows - asked, wide), F32)], 0)
+        blank = jnp.zeros((rows, span - wide), F32)
+        dt = (
+            jnp.concatenate([dq, blank], 1)
+            + turn(jnp.concatenate([dk, blank], 1), local)
+            + jnp.concatenate([blank, dv], 1)
+        ).astype(BF)
+        dt_s[g] = dt
+        g_qkv = dot_lt(mixer_in[...], dt)
+        if g >= 2:
+            ship(g - 2, 0, up).wait()
+        slot = wide_s.at[g % 2]
+        slot[:, : up - wide] = g_qkv[:, : up - wide]
+        slot[:, up - wide : span] = g_qkv[:, up - wide :] + g_o[:, : span - up + wide]
+        slot[:, span:up] = g_o[:, span - up + wide :]
+        ship(g, 0, up).start()
+
+    for g in range(groups):
+        attend_back(g)
+    grad_a = chain(lambda g: dot_rt(dt_s[g], bank[g, :, :span]), groups)
+    grad_start, g_first = norm_back_of(norm1[...], scale1[...], first, grad_a)
+    grad_start = (
+        grad_start + jnp.concatenate([grad_mid, jnp.zeros((rows - asked, grad_mid.shape[1]), F32)], 0)
     ).astype(BF)
-    ds_c, ds_t = (grad_scores[..., :nctx], grad_scores[..., nctx:])
-    p_c, p_t = (probs[..., :nctx], probs[..., nctx:])
-    root = size**-0.5
-    grad_q = (
-        (dots("ghbnm,gmhs->gbnhs", ds_c, k_c) + dots("ghbnm,gbmhs->gbnhs", ds_t, k_t)) * root
-    ).astype(BF)
-    grad_k_t = (dots("ghbnm,gbnhs->gbmhs", ds_t, q_b) * root).astype(BF)
-    grad_v_t = dots("ghbnm,gbnhs->gbmhs", p_t, gm).astype(BF)
-    grad_k_c = jnp.sum(
-        (dots("ghbnm,gbnhs->gbmhs", ds_c, q_b) * root).astype(BF).astype(F32), 1
-    )
-    grad_v_c = jnp.sum(dots("ghbnm,gbnhs->gbmhs", p_c, gm).astype(BF).astype(F32), 1)
-    kv_c = jnp.concatenate([merge_heads(grad_k_c), merge_heads(grad_v_c)], 2)
-    high = kv_c.astype(BF)
-    low = (kv_c - high.astype(F32)).astype(BF)
-    flat = (groups, asked, plocal)
-    t_rows = jnp.concatenate(
-        [grad_q.reshape(flat), grad_k_t.reshape(flat), grad_v_t.reshape(flat)], 2
-    )
-    a_c, a_t = (mixer_in[:nctx], mixer_in[nctx:])
-    g_q = dots("nd,gnk->gdk", a_t, t_rows[:, :, :plocal])
-    g_kv = dots(
-        "nd,gnk->gdk",
-        jnp.concatenate([a_c, a_c, a_t], 0),
-        jnp.concatenate([high, low, t_rows[:, :, plocal:]], 1),
-    )
-    w_kv = bank[:, :, plocal : 3 * plocal]
-    grad_a = jnp.concatenate(
-        [
-            dots("gnk,gdk->nd", high, w_kv) + dots("gnk,gdk->nd", low, w_kv),
-            dots("gnk,gdk->nd", t_rows, w_qkv),
+    small[...] = jnp.concatenate([g_first, g_second], 0)
+
+    def tail(g):
+        return pltpu.make_async_copy(
+            tail_s.at[g], grads.at[g, :, pl.ds(emb, wide)], sems.at[2 + g]
+        )
+
+    for g in range(groups):
+        tail_s[g] = dot_lt(grad_start, pix[g])
+        tail(g).start()
+    for g in range(groups - 2, groups):
+        ship(g, 0, up).wait()
+    for g in range(groups):
+        tail(g).wait()
+
+
+def run_encoder_back(grad_ctx, pix, saved, bank, gains, sizes):
+    local, hidden, size = sizes
+    groups, width, columns = bank.shape
+    rows = pix.shape[1]
+    make = jax.ShapeDtypeStruct
+    ins = [grad_ctx, pix, *saved, bank, gains]
+    vmem = pl.BlockSpec(memory_space=pltpu.VMEM)
+    return pl.pallas_call(
+        functools.partial(encoder_back_kernel, sizes),
+        out_shape=[make(bank.shape, F32), make((2, width), F32)],
+        in_specs=[vmem] * len(ins),
+        out_specs=[pl.BlockSpec(memory_space=pl.ANY), vmem],
+        scratch_shapes=[
+            pltpu.VMEM((2, width, 4 * local + 2 * hidden), F32),
+            pltpu.VMEM((groups, width, local + 64), F32),
+            pltpu.VMEM((groups, rows, 3 * local + 64), BF),
+            pltpu.SemaphoreType.DMA((2 + groups,)),
         ],
-        0,
-    )
-    grad_in, g_first = norm_back(norm1, scale1, first, grad_a)
-    g_token = jnp.sum(grad_in[nctx:] + grad_mid, 0)
-    grad_entry = grad_in[:nctx].astype(BF)
-    g_entry = dots("nd,gnk->gdk", grad_entry, spread)
-    grad_context = dots("nd,gdk->gnk", grad_entry, w_entry).transpose(1, 0, 2).reshape(nctx, -1)
-    g_bank = jnp.concatenate([g_q, g_kv, g_o, g_up, g_down, g_head, g_entry], 2)
-    return (grad_context, loss, g_bank, (g_first, g_second, g_final, g_token))
+        compiler_params=pltpu.CompilerParams(vmem_limit_bytes=58 * 2**20),
+    )(*ins)
 
 
 def per_device(
@@ -920,6 +1184,7 @@
     pix = lax.all_to_all(half, "mp", 0, 0, tiled=True)
     nctx = slots.shape[0]
     blocks, tlen = tslots.shape
+    rows = -(-patches // 16) * 16
 
     patch = jnp.arange(patches)
     hits = slots[:, None] == patch[None, :]
@@ -929,52 +1194,81 @@
         jnp.sum(jnp.where(hits, jnp.arange(nctx)[:, None], 0), 0),
         nctx + jnp.cumsum(1 - member.astype(jnp.int32)) - 1,
     )
-    shuffle = order[None, :] == patch[:, None]
-    places = jnp.sum(jnp.where(shuffle, patch[None, :], 0), 1)
+    shuffle = order[None, :] == jnp.arange(rows)[:, None]
+    places = jnp.sum(jnp.where(shuffle, patch[None, :] + 1, 0), 1) - 1
+    mixed_pix = jnp.einsum(
+        "jp,gpk->gjk", shuffle.astype(BF), pix, preferred_element_type=F32
+    ).astype(BF)
+
+    def widen(value):
+        return jnp.pad(value, ((0, 0), (0, rows - value.shape[1]), (0, 64)))
+
     ckeep = (jnp.arange(nctx) < count).astype(F32)
-    keep = (patch < count).astype(F32)
     tkeep = (jnp.arange(tlen)[None, :] < tcount[:, None]).astype(F32)
+    tflat = tslots.reshape(-1)
+    of_block = jnp.arange(blocks * tlen) // tlen
+    keys = jnp.concatenate(
+        [
+            jnp.broadcast_to(ckeep[None], (blocks * tlen, nctx)),
+            (of_block[:, None] == of_block[None, :]) * tkeep.reshape(1, -1),
+        ],
+        1,
+    )
 
     table = sincos(width)
-    sizes = (local, hidden, pixel)
-    t_out, _ = encoder_forward(
-        pix, table, jnp.ones_like(keep), tbank, (t_vec[:width], t_vec[width : 2 * width]),
-        sizes, patches,
-    )
-    t_norm = layer_stats(t_out)[0].astype(BF)
-    t_hot = (tslots.reshape(-1)[:, None] == patch[None, :]).astype(BF)
-    targets = jnp.dot(t_hot, t_norm, preferred_element_type=F32).astype(BF)
-
-    mixed_pix = dots("jp,gpk->gjk", shuffle.astype(BF), pix).astype(BF)
-    enc_gains = (s_vec[:width], s_vec[width : 2 * width])
-    latent, enc_saved = encoder_forward(
-        mixed_pix, pick(table, places), keep, bank, enc_gains, sizes, nctx
-    )
-    pv = s_vec[2 * width :]
-    pgains = (pv[:pwidth], pv[pwidth : 2 * pwidth], pv[2 * pwidth : 3 * pwidth], pv[3 * pwidth :])
-    grad_context, loss, g_pbank, p_small = predictor(
-        latent.astype(BF), targets, sincos(pwidth), slots, tslots, ckeep, tkeep, target_total,
-        pbank, pgains, (local, plocal, phidden),
-    )
-    g_bank, g_first, g_second = encoder_backward(
-        grad_context, enc_saved, mixed_pix, bank, enc_gains, sizes
-    )
-    g_vec = jnp.concatenate([g_first, g_second, *p_small])
-
-    small = g_vec.reshape(owners, groups, -1).transpose(1, 0, 2).reshape(groups, width, 1)
-    rest = jnp.zeros((groups, width, bank.shape[2] - extra - 1), F32)
-    g_bank = jnp.concatenate([g_bank, small, rest], 2)
-    r_bank, r_pbank, stats = reduce_all(
+    ptable = sincos(pwidth)
+    sizes = (local, hidden, width // HEADS)
+    slot_of = jnp.arange(rows)
+    hot = (tflat[:, None] == slot_of[None, :]).astype(BF)
+    (wanted,) = run_encoder(
+        widen(pix),
+        np.pad(table, ((0, rows - patches), (0, 0))),
+        (slot_of < patches).astype(F32),
+        tbank,
+        t_vec[: 2 * width].reshape(2, width),
+        sizes,
+        rows,
+        hot,
+    )
+    student_pix = widen(mixed_pix)
+    enc_gains = s_vec[: 2 * width].reshape(2, width)
+    context, *saved = run_encoder(
+        student_pix,
+        pick(table, places),
+        (slot_of < count).astype(F32),
+        bank,
+        enc_gains,
+        sizes,
+        nctx,
+    )
+    grad_context, g_pbank, p_small, loss = run_predictor(
+        context,
+        wanted,
+        pick(ptable, slots),
+        pick(ptable, tflat),
+        (keys - 1.0) * 1e9,
+        tkeep.reshape(-1, 1),
+        target_total.reshape(1, 1),
+        pbank,
+        s_vec[2 * width :].reshape(4, pwidth),
+        (local, plocal, phidden, pwidth // HEADS, blocks),
+    )
+    g_bank, e_small = run_encoder_back(grad_context, student_pix, saved, bank, enc_gains, sizes)
+    g_vec = jnp.concatenate([e_small.reshape(-1), p_small.reshape(-1)])
+    g_vec = g_vec.reshape(owners, groups, 1, -1).transpose(1, 0, 2, 3)
+    share = g_vec.shape[3]
+    r_bank, r_pbank, r_vec, stats = reduce_all(
         [
             g_bank.reshape(gathered[0].shape),
             g_pbank.reshape(gathered[1].shape),
+            jnp.pad(g_vec, ((0, 0), (0, 0), (0, 7), (0, -share % (2 * LANES)))),
         ],
-        (BF, F32),
-        jnp.broadcast_to(loss, (8, LANES)),
+        (BF, F32, F32),
+        loss,
     )
     r_pin, r_pout = unpack_predictor(r_pbank, local, plocal, phidden)
     r_in, r_out = unpack_encoder(r_bank, local, hidden, pixel)
-    r_vec = r_bank[:, extra]
+    r_vec = r_vec[0, :share]
     loss_total, squares = (stats[0, 0], stats[1, 0])
     grad_norm = jnp.sqrt(squares)
     scale = jnp.minimum(1.0, CLIP / (grad_norm + 1e-06))

time: 639 us -> 489 us (0.77)
  matrix products: 142 us -> 1.47 us
  Pallas kernels: 310 us -> 412 us
  local copies, waits for them, and re-layouts: 122 us -> 33.5 us
  other arithmetic: 47.7 us -> 29.1 us
    dot_general x62 -> x4, matrix products: 137 us -> 1.47 us  [the longest x3 1.13 us: pick(): rows = jnp.dot(hot, np.concatenate(parts, 1), preferred_element_type=F32)]
    pallas_call x0 -> x4, Pallas kernels: none -> 95.4 us  [the longest x1 34.4 us: run_predictor(): pl.pallas_call(functools.partial(predictor_kernel, sizes), out_shape=outs...]
    concatenate x4 -> x5, local copies, waits for them, and re-layouts: 45.9 us -> 0.89 us  [the longest x4 0.89 us: per_device(): g_vec = jnp.concatenate([e_small.reshape(-1), p_small.reshape(-1)])]
    sub x1, other arithmetic: 20.7 us -> 0.01 us  [per_device(): places = jnp.sum(jnp.where(shuffle, patch[None, :] + 1, 0), 1) - 1]
    transpose x3 -> x0, local copies, waits for them, and re-layouts: 14.5 us -> none  [dots(): return jnp.einsum(spec, left, right, preferred_element_type=F32)]
    reshape x16 -> x1, local copies, waits for them, and re-layouts: 12.2 us -> 0.01 us  [the longest x5 6.46 us: merge_heads(): return split.reshape(groups, rows, heads * size)]
    convert_element_type x8 -> x1, local copies, waits for them, and re-layouts: 8.61 us -> 0.2 us  [per_device(): mixed_pix = jnp.einsum('jp,gpk->gjk', shuffle.astype(BF), pix, preferred_...]
    unnamed x289 -> x72, local copies, waits for them, and re-layouts: 9.56 us -> 1.58 us
  transfers between devices with their start and end apart: 1 -> 1, of which waited for: 0 -> 0; matrix products, arithmetic and copies ran while one was open for 3% -> 8% of each run, Pallas kernels for 26% -> 33%
where the time goes in v3:
time: 489 us; the launch traced here: 485 us
  Pallas kernels  412 us (84%)
  local copies, waits for them, and re-layouts  33.5 us (7%)
  other arithmetic  29.1 us (6%)
  starting transfers between devices  5.16 us (1%)
    pallas_call x1, Pallas kernels, gather_all(): pl.pallas_call(functools.partial(gather_kernel, nz, count), out_shape=[ja...  162 us
    pallas_call x1, Pallas kernels, reduce_all(): pl.pallas_call(functools.partial(reduce_kernel, nz, count), out_shape=[ja...  155 us
    pallas_call x1, Pallas kernels, run_predictor(): pl.pallas_call(functools.partial(predictor_kernel, sizes), out_shape=outs...  34.4 us
    pallas_call x2, Pallas kernels, run_encoder(): pl.pallas_call(functools.partial(encoder_kernel, sizes, asked, saving), o...  31.7 us
    pallas_call x1, Pallas kernels, run_encoder_back(): pl.pallas_call(functools.partial(encoder_back_kernel, sizes), out_shape=[...  29.4 us
  transfers between devices with their start and end apart: 1, of which 0 were waited for; matrix products, arithmetic and copies ran while one was open for 8% of the time, Pallas kernels for 33%

profile of v3, /device:TPU:0, one launch (start us, length us, event | category | flops | bytes accessed | tf_op | source)
XLA Modules:
  0.0 485.2 jit_solution(10225075047105978557)
XLA Ops:
  0.7 1.4 copy-done
  2.9 5.2 %all-to-all-start = ((bf16[4,196,192]{1,2,0:T(8,128)(2,1)}), bf16[4,196,192]{1,2,0:T(8,128)(2,1)S(1)}, u32[]{:S(2)}, u32[]{:S(2)}) async-start(bf16[4,196,192]{1,2,0:T(8,128)(2,1)} %constant_dynamic-slice_fusion.2), calls=%async_computation | async-start | bytes 786432 | tf_op jit(solution)/shard_map/all_to_all | solution.py:1184
  10.6 1.1 convert.74
  11.8 1.0 convert_bitcast_fusion.1
  20.4 1.2 fusion.20.bias
  21.6 1.2 compare_convert_fusion.2
  28.3 1.0 slice_add_fusion.place
  32.3 1.0 concatenate.37.refs_2_
  33.3 1.0 concatenate.35.refs_0_
  34.3 162.1 %shard_map.418 = (bf16[4,8,96,2560]{3,2,1,0:T(8,128)(2,1)}, bf16[4,8,48,1536]{3,2,1,0:T(8,128)(2,1)}, bf16[4,8,96,2560]{3,2,1,0:T(8,128)(2,1)}) custom-call(bf16[96,2560]{1,0:T(8,128)(2,1)} %concatenate.35.refs_0_, bf16[48,1536]{1,0:T(8,128)(2,1)} %concatenate.36.refs_1_, bf16[96,2560]{1,0:T(8,128)(2,1)} %concatenate.37.refs_2_), custom_call_target="tpu_custom_call" | custom-call | tf_op jit(solution)/shard_map/pallas_call | solution.py:325
  196.4 1.6 convert_reduce_fusion
  197.9 1.7 slice_reduce_fusion.1
  200.4 1.7 slice_reduce_fusion
  206.7 1.0 fusion.1.bias
  210.9 15.7 %shard_map.419 = (bf16[4,160,256]{2,1,0:T(8,128)(2,1)}, f32[208,768]{1,0:T(8,128)}, f32[208,1]{1,0:T(8,128)}, bf16[208,768]{1,0:T(8,128)(2,1)}, bf16[4,160,256]{...) custom-call(bf16[4,208,256]{2,1,0:T(8,128)(2,1)} %pad.16.pix, ...), custom_call_target="tpu_custom_call" | custom-call | tf_op jit(solution)/shard_map/pallas_call | solution.py:789
  226.6 16.0 %shard_map.420.wanted = bf16[4,256,256]{2,1,0:T(8,128)(2,1)} custom-call(bf16[4,208,256]{2,1,0:T(8,128)(2,1)} %pad.17.pix, f32[208,768]{1,0:T(8,128)} %constant.81.clone.place, f32[1,208]{1,0:T(1,128)} %fusion.22.bias, bf16[4,768,2560]{2,1,0:T(8,128)(2,1)} %bitcast.63, f32[2,768]{1,0:T(2,128)} %reshape.244.gains, bf16[256,208]{1,0:T(8,128)(2,1)} %fusion.4.refs_0_), custom_call_target="tpu_custom_call" | custom-call | tf_op jit(solution)/shard_map/pallas_call | solution.py:789
  242.5 34.4 %shard_map.421 = (f32[160,768]{1,0:T(8,128)}, f32[4,384,1536]{2,1,0:T(8,128)}, f32[4,384]{1,0:T(4,128)}, f32[8,128]{1,0:T(8,128)}) custom-call(bf16[4,160,256]{2,1,0:T(8,128)(2,1)} %get-tuple-element.49.ctx, bf16[4,256,256]{2,1,0:T(8,128)(2,1)} %shard_map.420.wanted, f32[160,384]{1,0:T(8,128)} %slice_add_fusion.4.place_c, ...), custom_call_target="tpu_custom_call" | custom-call | tf_op jit(solution)/shard_map/pallas_call | solution.py:993
  276.9 29.4 %shard_map.422 = (f32[4,768,2560]{2,1,0:T(8,128)}, f32[2,768]{1,0:T(2,128)}) custom-call(f32[160,768]{1,0:T(8,128)} %get-tuple-element.53.grad_ctx, bf16[4,208,256]{2,1,0:T(8,128)(2,1)} %pad.16.pix, f32[208,768]{1,0:T(8,128)} %get-tuple-element.54.norm1, f32[208,1]{1,0:T(8,128)} %get-tuple-element.55.scale1, bf16[208,768]{1,0:T(8,128)(2,1)} %get-tuple-element.56.mixer_in, ...), custom_call_target="tpu_custom_call" | custom-call | tf_op jit(solution)/shard_map/pallas_call | solution.py:1110
  308.0 154.6 %shard_map.423 = (f32[96,2560]{1,0:T(8,128)}, f32[48,1536]{1,0:T(8,128)}, f32[8,256]{1,0:T(8,128)}, f32[8,128]{1,0:T(8,128)}) custom-call(f32[8,128]{1,0:T(8,128)} %get-tuple-element.52.stats_in, f32[4,8,96,2560]{3,2,1,0:T(8,128)} %bitcast.61, f32[4,8,48,1536]{3,2,1,0:T(8,128)} %bitcast.64, f32[4,8,8,256]{3,2,1,0:T(8,128)} %pad.18.refs_2_), custom_call_target="tpu_custom_call" | custom-call | tf_op jit(solution)/shard_map/pallas_call | solution.py:619
  462.6 1.6 fusion.35
  464.2 1.6 fusion.34
  465.8 1.4 slice.232
  467.2 1.5 slice.228
  468.7 1.1 fusion.32
  469.8 1.1 fusion.33
  470.9 1.7 slice.222
  472.5 1.3 fusion.38
  474.8 1.4 multiply_add_fusion.5
  476.2 2.7 multiply_add_fusion.2
  478.9 3.0 multiply_add_fusion
  482.0 0.9 multiply_subtract_fusion.3
  483.0 1.0 multiply_subtract_fusion.2
  (152 shorter events, 29.1 us)
Async XLA Ops:
  0.7 27.2 %copy-start.7 = (bf16[196,2304]{1,0:T(8,128)(2,1)S(1)}, bf16[196,2304]{1,0:T(8,128)(2,1)}, u32[]{:S(2)}) copy-start(bf16[196,2304]{1,0:T(8,128)(2,1)} %constant.84.clone) | copy-start | bytes 2709508
  0.7 16.9 %copy-start.2 = (f32[96,1344]{1,0:T(8,128)S(1)}, f32[96,1344]{1,0:T(8,128)}, u32[]{:S(2)}) copy-start(f32[96,1344]{1,0:T(8,128)} %param.47) | copy-start | bytes 1548292
  0.7 17.1 %copy-start.6 = (f32[1152,96]{0,1:T(8,128)S(1)}, f32[1152,96]{0,1:T(8,128)}, u32[]{:S(2)}) copy-start(f32[1152,96]{0,1:T(8,128)} %param.48) | copy-start | bytes 1327108
  0.7 22.1 %copy-start.29 = (s32[8,4]{0,1:T(4,128)S(1)}, s32[8,4]{0,1:T(4,128)}, u32[]{:S(2)}) copy-start(s32[8,4]{0,1:T(4,128)} %param.31) | copy-start | bytes 388
  2.9 205.6 %all-to-all-start = ((bf16[4,196,192]{1,2,0:T(8,128)(2,1)}), bf16[4,196,192]{1,2,0:T(8,128)(2,1)S(1)}, u32[]{:S(2)}, u32[]{:S(2)}) async-start(bf16[4,196,192]{1,2,0:T(8,128)(2,1)} %constant_dynamic-slice_fusion.2), calls=%async_computation | async-start | bytes 786432 | tf_op jit(solution)/shard_map/all_to_all | solution.py:1184
  8.0 11.8 %copy-start.35 = (s32[8]{0:T(128)S(1)}, s32[8]{0:T(128)}, u32[]{:S(2)}) copy-start(s32[8]{0:T(128)} %param.29) | copy-start | bytes 100
  18.6 13.0 %copy-start.19 = (bf16[48,288]{1,0:T(8,128)(2,1)S(1)}, bf16[48,288]{1,0:T(8,128)(2,1)}, u32[]{:S(2)}) copy-start(bf16[48,288]{1,0:T(8,128)(2,1)} %slice.247) | copy-start | bytes 82948
  18.6 13.0 %copy-start.20 = (bf16[48,384]{1,0:T(8,128)(2,1)S(1)}, bf16[48,384]{1,0:T(8,128)(2,1)}, u32[]{:S(2)}) copy-start(bf16[48,384]{1,0:T(8,128)(2,1)} %slice.249) | copy-start | bytes 110596
  18.6 12.9 %copy-start.21 = (bf16[48,384]{1,0:T(8,128)(2,1)S(1)}, bf16[48,384]{1,0:T(8,128)(2,1)}, u32[]{:S(2)}) copy-start(bf16[48,384]{1,0:T(8,128)(2,1)} %slice.250) | copy-start | bytes 110596
  18.6 12.9 %copy-start.23 = (bf16[48,96]{1,0:T(8,128)(2,1)S(1)}, bf16[48,96]{1,0:T(8,128)(2,1)}, u32[]{:S(2)}) copy-start(bf16[48,96]{1,0:T(8,128)(2,1)} %slice.248) | copy-start | bytes 27652
  18.6 13.7 %copy-start.13 = (bf16[96,192]{1,0:T(8,128)(2,1)S(1)}, bf16[96,192]{1,0:T(8,128)(2,1)}, u32[]{:S(2)}) copy-start(bf16[96,192]{1,0:T(8,128)(2,1)} %get-tuple-element.104) | copy-start | bytes 110596
  28.3 176.0 %copy-start.4 = (bf16[196,1152]{1,0:T(8,128)(2,1)S(1)}, bf16[196,1152]{1,0:T(8,128)(2,1)}, u32[]{:S(2)}) copy-start(bf16[196,1152]{1,0:T(8,128)(2,1)} %constant.85.clone) | copy-start | bytes 1354756
  28.3 176.0 %copy-start.25 = (s32[1,160]{1,0:T(1,128)S(1)}, s32[1,160]{1,0:T(1,128)}, u32[]{:S(2)}) copy-start(s32[1,160]{1,0:T(1,128)} %copy-done.24) | copy-start | bytes 1924
  33.3 173.3 %copy-start.27 = (s32[256]{0:T(256)S(1)}, s32[256]{0:T(256)}, u32[]{:S(2)}) copy-start(s32[256]{0:T(256)} %and_select_fusion) | copy-start | bytes 3076
  33.3 173.3 %copy-start.28 = (f32[256]{0:T(256)S(1)}, f32[256]{0:T(256)}, u32[]{:S(2)}) copy-start(f32[256]{0:T(256)} %reshape.245) | copy-start | bytes 3076
  33.3 173.4 %copy-start.30 = (f32[160]{0:T(256)S(1)}, f32[160]{0:T(256)}, u32[]{:S(2)}) copy-start(f32[160]{0:T(256)} %compare_convert_fusion.2) | copy-start | bytes 1924
  276.9 30.2 %copy-start.26 = (f32[4,384]{1,0:T(4,128)S(1)}, f32[4,384]{1,0:T(4,128)}, u32[]{:S(2)}) copy-start(f32[4,384]{1,0:T(4,128)} %get-tuple-element.70) | copy-start | bytes 18436
  308.0 166.8 %copy-start.31 = (f32[96]{0:T(128)S(1)}, f32[96]{0:T(128)}, u32[]{:S(2)}) copy-start(f32[96]{0:T(128)} %param.36) | copy-start | bytes 1156
  308.0 166.8 %copy-start.32 = (f32[96]{0:T(128)S(1)}, f32[96]{0:T(128)}, u32[]{:S(2)}) copy-start(f32[96]{0:T(128)} %param.49) | copy-start | bytes 1156
  308.0 166.8 %copy-start.33 = (f32[96]{0:T(128)S(1)}, f32[96]{0:T(128)}, u32[]{:S(2)}) copy-start(f32[96]{0:T(128)} %param.41) | copy-start | bytes 1156
  308.0 166.8 %copy-start.34 = (f32[96]{0:T(128)S(1)}, f32[96]{0:T(128)}, u32[]{:S(2)}) copy-start(f32[96]{0:T(128)} %param.46) | copy-start | bytes 1156
  308.0 168.2 %copy-start.5 = (f32[1152,96]{0,1:T(8,128)S(1)}, f32[1152,96]{0,1:T(8,128)}, u32[]{:S(2)}) copy-start(f32[1152,96]{0,1:T(8,128)} %param.33) | copy-start | bytes 1327108
  462.6 16.3 %copy-start.3 = (f32[96,1344]{1,0:T(8,128)S(1)}, f32[96,1344]{1,0:T(8,128)}, u32[]{:S(2)}) copy-start(f32[96,1344]{1,0:T(8,128)} %param.32) | copy-start | bytes 1548292
  474.7 7.3 %copy-start.9 = (f32[672,48]{0,1:T(8,128)S(1)}, f32[672,48]{0,1:T(8,128)}, u32[]{:S(2)}) copy-start(f32[672,48]{0,1:T(8,128)} %param.35) | copy-start | bytes 387076
  474.7 7.3 %copy-start.12 = (f32[48,384]{1,0:T(8,128)S(1)}, f32[48,384]{1,0:T(8,128)}, u32[]{:S(2)}) copy-start(f32[48,384]{1,0:T(8,128)} %get-tuple-element.101) | copy-start | bytes 221188
  474.7 7.3 %copy-start.14 = (f32[48,192]{1,0:T(8,128)S(1)}, f32[48,192]{1,0:T(8,128)}, u32[]{:S(2)}) copy-start(f32[48,192]{1,0:T(8,128)} %get-tuple-element.99) | copy-start | bytes 110596
  474.7 7.3 %copy-start.17 = (f32[672,48]{0,1:T(8,128)S(1)}, f32[672,48]{0,1:T(8,128)}, u32[]{:S(2)}) copy-start(f32[672,48]{0,1:T(8,128)} %param.40) | copy-start | bytes 387076
  474.7 7.3 %copy-start.18 = (f32[672,48]{0,1:T(8,128)S(1)}, f32[672,48]{0,1:T(8,128)}, u32[]{:S(2)}) copy-start(f32[672,48]{0,1:T(8,128)} %param.45) | copy-start | bytes 387076
  474.7 7.3 %copy-start.22 = (f32[48,96]{1,0:T(8,128)S(1)}, f32[48,96]{1,0:T(8,128)}, u32[]{:S(2)}) copy-start(f32[48,96]{1,0:T(8,128)} %slice.232) | copy-start | bytes 55300
  474.8 9.2 %copy-start.1 = (bf16[8,196,192]{1,2,0:T(8,128)(2,1)S(1)}, bf16[8,196,192]{1,2,0:T(8,128)(2,1)}, u32[]{:S(2)}) copy-start(bf16[8,196,192]{1,2,0:T(8,128)(2,1)} %param.27) | copy-start | bytes 1806340
  476.2 6.7 %copy-start.8 = (f32[48,864]{1,0:T(8,128)S(1)}, f32[48,864]{1,0:T(8,128)}, u32[]{:S(2)}) copy-start(f32[48,864]{1,0:T(8,128)} %param.34) | copy-start | bytes 497668
  476.2 6.7 %copy-start.10 = (f32[48,288]{1,0:T(8,128)S(1)}, f32[48,288]{1,0:T(8,128)}, u32[]{:S(2)}) copy-start(f32[48,288]{1,0:T(8,128)} %slice.228) | copy-start | bytes 165892
  (5 other events, 23.0 us)
